TPU v7x, 32 devices: a whole 2x2x4 slice. The times are simulated.
32 devices in a mesh: fsdp: 8 (over y, x, core), tensor: 4 (over z).
Axes of the slice: x: 2, y: 2, z: 4, core: 2. Of those that a mesh axis runs over, the one named last changes fastest.
Arguments:
- tokens: bfloat16 [1024, 8192], P('tensor', 'fsdp'), may hold values from -6 to 6
- gate_weight: bfloat16 [8192, 14336], P('fsdp', 'tensor'), may hold values from -0.0625 to 0.0625
- up_weight: bfloat16 [8192, 14336], P('fsdp', 'tensor'), may hold values from -0.0625 to 0.0625
- down_frozen: bfloat16 [14336, 8192], P('tensor', 'fsdp'), may hold values from -0.046875 to 0.046875
- down_learn: bfloat16 [14336, 8192], P('tensor', 'fsdp'), may hold values from -0.046875 to 0.046875
- steer: float32 [8192], replicated, may hold values from -6 to 6
- sample_lengths: int32 [2, 4], replicated, may hold values from 1 to 128, 320 in all within a row
Outputs:
- grad_down: float32 [14336, 8192], P('tensor', 'fsdp')
- losses: float32 [2], replicated
Inputs may be any that keep to these rules, and one draw needn't show every extreme that they name: `sample_lengths`: in each row, the lengths sum to 320 and one sample has exactly 128 live tokens.
All inputs are finite; a program needn't handle non-finite values.
Results may differ from a plain program's by a relative error of at most 0.0047.
Values may be sent and summed in bfloat16 or wider, within the bound.
No kernel may reach another device: no remote copies, remote signals or barrier semaphores. Data moves between devices by JAX's collectives and lax.ppermute only.
A program may use at most 128 MiB of HBM per device.

v0:
```python
import jax
import jax.numpy as jnp
from jax import lax
from jax.sharding import PartitionSpec as P

D = 8192
SLOT = 128


def slot_lengths(slot_ids, flat, sample_count):
    sample_ids = jnp.arange(sample_count, dtype=jnp.int32)
    return jnp.sum(jnp.where(slot_ids[:, None] == sample_ids[None, :], flat[None, :], 0), axis=1)


def shards(tokens, gate_weight, up_weight, down_frozen, down_learn, steer, sample_lengths):
    rows_tp = tokens.shape[0]
    cols = tokens.shape[1]
    width_ff = gate_weight.shape[1]
    n_tensor = lax.axis_size("tensor")
    total_rows = rows_tp * n_tensor
    seq_count = sample_lengths.shape[1]
    flat = sample_lengths.reshape(-1)
    gathered = lax.all_gather(tokens, "tensor", axis=0, tiled=True)
    every_slot = jnp.arange(total_rows, dtype=jnp.int32)
    every_len = slot_lengths(every_slot // SLOT, flat, 2 * seq_count)
    dead_key = jnp.where(every_slot % SLOT < every_len, 0, 1).astype(jnp.int32)
    live_total = 2 * (seq_count * SLOT * 5 // 8)
    source_ids = jnp.argsort(dead_key, stable=True)[:live_total]
    work_rows = jnp.take(gathered, source_ids, axis=0)
    count_rows = work_rows.shape[0]
    both_in = jnp.concatenate([gate_weight, up_weight], axis=1)
    block = work_rows
    summed = lax.psum_scatter(
        jnp.dot(block, both_in, preferred_element_type=jnp.float32),
        "fsdp",
        scatter_dimension=0,
        tiled=True,
    )
    hidden_own = (jax.nn.silu(summed[:, :width_ff]) * summed[:, width_ff:]).astype(jnp.bfloat16)
    hidden_all = lax.all_gather(hidden_own, "fsdp", axis=0, tiled=True)
    both_out = jnp.concatenate([down_frozen, down_learn], axis=1)
    own_count = count_rows // n_tensor
    block = hidden_all
    mlp_terms = lax.psum_scatter(
        jnp.dot(block, both_out, preferred_element_type=jnp.float32),
        "tensor",
        scatter_dimension=0,
        tiled=True,
    )
    own_start = lax.axis_index("tensor") * own_count
    base = lax.dynamic_slice_in_dim(work_rows, own_start, own_count, 0).astype(jnp.float32)
    out_frozen = base + mlp_terms[:, :cols]
    out_learn = base + mlp_terms[:, cols:]
    row_ids = lax.dynamic_slice_in_dim(source_ids, own_start, own_count, 0)
    row_len = slot_lengths(row_ids // SLOT, flat, 2 * seq_count)
    live = row_ids % SLOT < row_len
    forget = (live & (row_ids < seq_count * SLOT))[:, None]
    retain = (live & (row_ids >= seq_count * SLOT))[:, None]
    scale = 20.0 / jnp.sqrt(D * (jnp.mean(steer * steer) + 1e-06))
    target = scale * lax.dynamic_slice_in_dim(steer, lax.axis_index("fsdp") * cols, cols)
    steer_diff = out_learn - target[None, :]
    keep_diff = out_learn - out_frozen
    zero = jnp.zeros((), jnp.float32)
    local_steer = jnp.sum(jnp.where(forget, steer_diff * steer_diff, zero))
    local_keep = jnp.sum(jnp.where(retain, keep_diff * keep_diff, zero))
    sum_steer, sum_keep = lax.psum((local_steer, local_keep), ("fsdp", "tensor"))
    count_f = jnp.sum(sample_lengths[0]).astype(jnp.float32)
    count_r = jnp.sum(sample_lengths[1]).astype(jnp.float32)
    losses = jnp.stack([sum_steer / (count_f * D), sum_keep / (count_r * D)])
    delta = (jnp.where(forget, steer_diff, zero) + 2.0 * jnp.where(retain, keep_diff, zero)).astype(
        jnp.bfloat16
    )
    delta_all = lax.all_gather(delta, "tensor", axis=0, tiled=True)
    grad_down = lax.dot_general(
        hidden_all, delta_all, (((0,), (0,)), ((), ())), preferred_element_type=jnp.float32
    )
    return (grad_down, losses)


def solution(mesh):
    return jax.shard_map(
        shards,
        mesh=mesh,
        in_specs=(
            P("tensor", "fsdp"),
            P("fsdp", "tensor"),
            P("fsdp", "tensor"),
            P("tensor", "fsdp"),
            P("tensor", "fsdp"),
            P(),
            P(),
        ),
        out_specs=(P("tensor", "fsdp"), P()),
        check_vma=False,
    )
```

profile of v0, /device:TPU:0, one launch (start us, length us, event | category | flops | bytes accessed | tf_op | source)
XLA Modules:
  0.0 421.3 jit_solution(2584339748548459881)
XLA Ops:
  7.2 0.0 all-gather.4.cloned.1.call-start
  7.2 0.7 all-gather.4.cloned.1.call-update
  7.9 0.0 reduce-scatter.3.cloned.1.call-start
  7.9 0.8 broadcast_in_dim.75
  8.7 0.1 select_reduce_fusion.2
  8.8 4.4 %sort.17 = (s32[1024]{0:T(1024)}, s32[1024]{0:T(1024)S(1)}) sort(s32[1024]{0:T(1024)S(1)} %fusion.16, s32[1024]{0:T(1024)S(1)} %iota.21), dimensions={0}, to_apply=%region_1.2 | sort | flops 10240 | bytes 16384 | tf_op jit(solution)/shard_map/jit(argsort)/sort | solution.py:28
  13.2 45.1 %all-gather.4.cloned.1.call-done = bf16[1024,1024]{1,0:T(8,128)(2,1)} async-done(((bf16[256,1024]{1,0:T(8,128)(2,1)}), bf16[1024,1024]{1,0:T(8,128)(2,1)}) %all-gather.4.cloned.1.call-update) | async-done | bytes 2097168 | tf_op jit(solution)/shard_map/all_gather | solution.py:23
  58.3 5.7 %gather_fusion = bf16[640,1024]{1,0:T(8,128)(2,1)S(1)} fusion(bf16[1024,1024]{1,0:T(8,128)(2,1)} %all-gather.4.cloned.1.call-done, s32[1024]{0:T(1024)S(1)} %pad_clamp_fusion), kind=kCustom, calls=%fused_computation | custom fusion | bytes 2624000 | tf_op jit(solution)/shard_map/jit(_take)/gather | solution.py:29
  64.0 0.2 broadcast_select_fusion
  64.2 16.7 %fusion = f32[640,7168]{1,0:T(8,128)} fusion(bf16[640,1024]{1,0:T(8,128)(2,1)S(1)} %broadcast_select_fusion, bf16[1024,3584]{1,0:T(8,128)(2,1)} %param.9, bf16[1024,3584]{1,0:T(8,128)(2,1)} %param.8), kind=kOutput, calls=%fused_computation.1 | convolution fusion | flops 9424601088 | bytes 34340864 | tf_op jit(solution)/shard_map/dot_general | solution.py:34
  80.9 0.0 reduce-scatter.3.cloned.1.call-update
  80.9 0.0 all-gather.6.cloned.1.call-start
  81.0 122.1 %reduce-scatter.3.cloned.1.call-done = f32[80,7168]{1,0:T(8,128)} async-done(((f32[640,7168]{1,0:T(8,128)}), f32[80,7168]{1,0:T(8,128)}) %reduce-scatter.3.cloned.1.call-update) | async-done | bytes 2293776 | tf_op jit(solution)/shard_map/reduce_scatter | solution.py:33
  203.1 2.7 fusion.8
  205.8 0.0 all-gather.6.cloned.1.call-update
  205.8 0.0 reduce-scatter.5.cloned.1.call-start
  205.9 38.5 %all-gather.6.cloned.1.call-done = bf16[640,3584]{1,0:T(8,128)(2,1)} async-done(((bf16[80,3584]{1,0:T(8,128)(2,1)}), bf16[640,3584]{1,0:T(8,128)(2,1)}) %all-gather.6.cloned.1.call-update) | async-done | bytes 4587536 | tf_op jit(solution)/shard_map/all_gather | solution.py:40
  244.4 15.9 %fusion.4 = f32[640,2048]{1,0:T(8,128)} fusion(bf16[640,3584]{1,0:T(8,128)(2,1)} %all-gather.6.cloned.1.call-done, bf16[3584,1024]{1,0:T(8,128)(2,1)} %param.11, bf16[3584,1024]{1,0:T(8,128)(2,1)} %param.10), kind=kOutput, calls=%fused_computation.5 | convolution fusion | flops 9424601088 | bytes 24510464 | tf_op jit(solution)/shard_map/dot_general | solution.py:45
  260.2 0.0 reduce-scatter.5.cloned.1.call-update
  260.2 0.2 all-gather.8.cloned.1.call-start
  260.5 0.5 copy-done
  261.0 0.6 multiply_reduce_fusion
  262.3 0.1 and_select_fusion
  262.4 0.1 select_reduce_fusion.3
  262.5 0.1 compare_and_fusion.2
  262.5 0.1 compare_and_fusion.1
  262.6 91.6 %reduce-scatter.5.cloned.1.call-done = f32[160,2048]{1,0:T(8,128)} async-done(((f32[640,2048]{1,0:T(8,128)}), f32[160,2048]{1,0:T(8,128)}) %reduce-scatter.5.cloned.1.call-update) | async-done | bytes 1310736 | tf_op jit(solution)/shard_map/reduce_scatter | solution.py:44
  354.2 3.0 select_reduce_fusion.1
  357.2 0.7 slice_reduce_fusion.1
  359.0 42.2 %all-reduce = (f32[]{:T(128)}, f32[]{:T(128)}) all-reduce(f32[]{:T(128)} %get-tuple-element.5, f32[]{:T(128)} %get-tuple-element.4), channel_id=1, replica_groups=mesh['fsdp'=8,'tensor'=4] {'fsdp','tensor'}, use_global_device_ids=true, to_apply=%region_10.11 | all-reduce | flops 2 | bytes 16 | tf_op jit(solution)/shard_map/psum | solution.py:66
  402.5 0.6 pad_maximum_fusion
  403.1 11.7 %fusion.22 = f32[3584,1024]{1,0:T(8,128)} fusion(bf16[640,3584]{1,0:T(8,128)(2,1)} %all-gather.6.cloned.1.call-done, bf16[640,1024]{1,0:T(8,128)(2,1)} %all-gather.8.cloned.1.call-done), kind=kOutput, calls=%fused_computation.55 | convolution fusion | flops 4697620480 | bytes 20578304 | tf_op jit(solution)/shard_map/dot_general | solution.py:74
  (12 shorter events, 0.1 us)
Async XLA Ops:
  7.2 51.1 %all-gather.4.cloned.1.call-start = ((), (), s32[]{:S(2)}) async-start(), calls=%async_computation.2 | async-start | bytes 2621440 | tf_op jit(solution)/shard_map/all_gather | solution.py:23
  7.9 195.2 %reduce-scatter.3.cloned.1.call-start = ((), (), s32[]{:S(2)}) async-start(), calls=%async_computation.3 | async-start | bytes 20643840 | tf_op jit(solution)/shard_map/reduce_scatter | solution.py:33
  80.9 163.4 %all-gather.6.cloned.1.call-start = ((), (), s32[]{:S(2)}) async-start(), calls=%async_computation.4 | async-start | bytes 5160960 | tf_op jit(solution)/shard_map/all_gather | solution.py:40
  205.8 148.3 %reduce-scatter.5.cloned.1.call-start = ((), (), s32[]{:S(2)}) async-start(), calls=%async_computation.5 | async-start | bytes 6553600 | tf_op jit(solution)/shard_map/reduce_scatter | solution.py:44
  260.2 0.8 copy-start
  260.2 97.0 %copy-start.1 = (s32[2,4]{1,0:T(2,128)S(1)}, s32[2,4]{1,0:T(2,128)}, u32[]{:S(2)}) copy-start(s32[2,4]{1,0:T(2,128)} %param.13) | copy-start | bytes 100
  260.2 142.8 %all-gather.8.cloned.1.call-start = ((), (), s32[]{:S(2)}) async-start(), calls=%async_computation.6 | async-start | bytes 1638400 | tf_op jit(solution)/shard_map/all_gather | solution.py:73
Sparse Core Ops, SparseCore 0:
  9.6 48.6 all-gather.3
  81.1 121.9 reduce-scatter.2
  206.0 38.3 all-gather.5
  260.4 93.7 reduce-scatter.4
  357.3 34.1 all-gather.7
where the time goes:
time: 422 us; the launch traced here: 421 us
  waiting for transfers between devices  298 us (71%)
  matrix products  44.2 us (10%)
  blocking collectives  42.2 us (10%)
  between operations  16.9 us (4%)
  other arithmetic  12.6 us (3%)
  local copies, waits for them, and re-layouts  7 us (2%)
    reduce_scatter x1, waiting for transfers between devices, shards(): lax.psum_scatter(jnp.dot(block, both_in, preferred_element_type=jnp.float...  122 us
    reduce_scatter x1, waiting for transfers between devices, shards(): lax.psum_scatter(jnp.dot(block, both_out, preferred_element_type=jnp.floa...  91.6 us
    all_gather x1, waiting for transfers between devices, shards(): gathered = lax.all_gather(tokens, 'tensor', axis=0, tiled=True)  45.1 us
    psum x1, blocking collectives, shards(): lax.psum((local_steer, local_keep), ('fsdp', 'tensor'))  42.2 us
    all_gather x1, waiting for transfers between devices, shards(): hidden_all = lax.all_gather(hidden_own, 'fsdp', axis=0, tiled=True)  38.5 us
    dot_general x1, matrix products, shards(): jnp.dot(block, both_in, preferred_element_type=jnp.float32)  16.7 us
    dot_general x1, matrix products, shards(): jnp.dot(block, both_out, preferred_element_type=jnp.float32)  15.9 us
    dot_general x1, matrix products, shards(): lax.dot_general(hidden_all, delta_all, (((0,), (0,)), ((), ())), preferre...  11.7 us
  transfers between devices with their start and end apart: 5, of which 4 were waited for; matrix products, arithmetic and copies ran while one was open for 2% of the time, Pallas kernels for 0%

commit v1 on v0

--- a/solution.py
+++ b/solution.py
@@ -1,10 +1,24 @@
+import math
+
 import jax
 import jax.numpy as jnp
 from jax import lax
+from jax.experimental import pallas as pl
+from jax.experimental.pallas import tpu as pltpu
 from jax.sharding import PartitionSpec as P
 
 D = 8192
 SLOT = 128
+TOKEN_BOUND = 6.0
+WEIGHT_BOUND = 0.0625
+HALF_MAX = 65504.0
+VMEM_BYTES = 8 * 1024 * 1024
+IN_VMEM_BYTES = 50 * 1024 * 1024
+f32 = jnp.float32
+bf16 = jnp.bfloat16
+f16 = jnp.float16
+FIRST = (2, 4)
+SECOND = (4, 2)
 
 
 def slot_lengths(slot_ids, flat, sample_count):
@@ -12,7 +26,272 @@
     return jnp.sum(jnp.where(slot_ids[:, None] == sample_ids[None, :], flat[None, :], 0), axis=1)
 
 
-def shards(tokens, gate_weight, up_weight, down_frozen, down_learn, steer, sample_lengths):
+def dot(a, b):
+    return jnp.dot(a, b, preferred_element_type=f32)
+
+
+def swap(axis, bit, x):
+    return lax.ppermute(x, axis, [(i, i ^ bit) for i in range(lax.axis_size(axis))])
+
+
+def by_core(axis_bits, x):
+    even, odd = axis_bits
+    n = lax.axis_size("fsdp")
+    return lax.ppermute(x, "fsdp", [(i, i ^ (odd if i % 2 else even)) for i in range(n)])
+
+
+def after(x, *others):
+    return lax.optimization_barrier((x,) + others)[0]
+
+
+def in_kernel(core_ref, x1_ref, x2_ref, s1_ref, s2_ref, wg_ref, wu_ref, sg_ref, su_ref, out_ref, *, scale):
+    x = jnp.concatenate([x1_ref[...], x2_ref[...]], axis=0)
+    xs = jnp.concatenate([s1_ref[...], s2_ref[...]], axis=0)
+    out_ref[0] = (dot(x, wg_ref[...]) + dot(xs, sg_ref[...])) * scale
+    out_ref[1] = (dot(x, wu_ref[...]) + dot(xs, su_ref[...])) * scale
+
+
+def in_products(core, first, first_at, second, second_at, weights, quarter, scale):
+    gate_weight, up_weight, gate_sib, up_sib = weights
+    cols, half = gate_sib.shape
+    steps = 2
+    tile = half // steps
+    rows1 = pl.BlockSpec((quarter, cols), lambda j, c: (first_at(c[0]), 0))
+    rows2 = pl.BlockSpec((quarter, cols), lambda j, c: (second_at(c[0]), 0))
+    own = pl.BlockSpec((cols, tile), lambda j, c: (0, c[0] * steps + j))
+    sib = pl.BlockSpec((cols, tile), lambda j, c: (0, j))
+    return pl.pallas_call(
+        lambda *refs: in_kernel(*refs, scale=scale),
+        grid_spec=pltpu.PrefetchScalarGridSpec(
+            num_scalar_prefetch=1,
+            grid=(steps,),
+            in_specs=[rows1, rows2, rows1, rows2, own, own, sib, sib],
+            out_specs=pl.BlockSpec((2, 2 * quarter, tile), lambda j, c: (0, 0, j)),
+        ),
+        out_shape=jax.ShapeDtypeStruct((2, 2 * quarter, half), f32),
+        compiler_params=pltpu.CompilerParams(vmem_limit_bytes=IN_VMEM_BYTES),
+        name="in_products",
+    )(core, first[0], second[0], first[1], second[1], gate_weight, up_weight, gate_sib, up_sib)
+
+
+def turn_kernel(*refs):
+    *parts, out_ref = refs
+    out_ref[...] = jnp.concatenate([p[...] for p in parts], axis=0).T
+
+
+def turned(parts):
+    width = parts[0].shape[1]
+    rows = sum(p.shape[0] for p in parts)
+    tile = 512
+    return pl.pallas_call(
+        turn_kernel,
+        grid=(width // tile,),
+        in_specs=[pl.BlockSpec((p.shape[0], tile), lambda j: (0, j)) for p in parts],
+        out_specs=pl.BlockSpec((tile, rows), lambda j: (j, 0)),
+        out_shape=jax.ShapeDtypeStruct((width, rows), bf16),
+        compiler_params=pltpu.CompilerParams(vmem_limit_bytes=VMEM_BYTES),
+        name="turned",
+    )(*parts)
+
+
+def paired_shards(tokens, gate_weight, up_weight, down_frozen, down_learn, steer, sample_lengths):
+    cols = tokens.shape[1]
+    slots = tokens.shape[0]
+    half = gate_weight.shape[1] // 2
+    seqs = sample_lengths.shape[1]
+    rows = seqs * SLOT * 5 // 8
+    own_rows, quarter = rows // 2, rows // 4
+    total = cols * lax.axis_size("fsdp")
+    scale = 2.0 ** math.floor(math.log2(HALF_MAX / (TOKEN_BOUND * WEIGHT_BOUND * total)))
+    me_f = lax.axis_index("fsdp")
+    me_t = lax.axis_index("tensor")
+    core = me_f % 2
+    chip = me_f // 2
+    forget_first = me_t // 2 == 0
+    low_half = (me_t % 2) == (me_t // 2)
+    even = core == 0
+    core_arg = core.reshape(1).astype(jnp.int32)
+
+    other_tokens = swap("tensor", 1, tokens)
+
+    def given(w):
+        return lax.dynamic_slice_in_dim(w, (1 - core) * half, half, 1)
+
+    gate_give = given(gate_weight)
+    gate_sib = swap("fsdp", 1, gate_give)
+    up_give = given(after(up_weight, gate_give))
+    up_sib = swap("fsdp", 1, up_give)
+    weights = (gate_weight, up_weight, gate_sib, up_sib)
+
+    lengths = jnp.where(forget_first, sample_lengths[0], sample_lengths[1])
+    before = jnp.cumsum(lengths) - lengths
+
+    def pick(block_of_slots):
+        slot_ids = block_of_slots * slots + jnp.arange(slots, dtype=jnp.int32)
+        sample = slot_ids // SLOT
+        inside = slot_ids % SLOT
+        position = slot_lengths(sample, before, seqs) + inside
+        position = jnp.where(inside < slot_lengths(sample, lengths, seqs), position, -1)
+        row = jnp.arange(rows, dtype=jnp.int32)
+        wanted = jnp.bitwise_xor(chip, row // quarter) * quarter + row % quarter
+        return (wanted[:, None] == position[None, :]).astype(bf16)
+
+    mine = me_t % 2
+    mine_rows = dot(pick(mine), after(tokens, up_give))
+    other_tokens = after(other_tokens, up_give, mine_rows)
+    x_a = (mine_rows + dot(pick(1 - mine), other_tokens)).astype(bf16)
+    hi_a, lo_a = x_a[quarter:], x_a[:quarter]
+    hi_b = swap("tensor", 3, hi_a)
+    lo_b = swap("tensor", 3, lo_a)
+    frozen_a = jnp.where(forget_first, 0.0, 1.0)
+    frozen_b = 1.0 - frozen_a
+    latest = []
+
+    def go(*xs):
+        out = lax.optimization_barrier(xs + tuple(latest))[: len(xs)]
+        return out[0] if len(xs) == 1 else out
+
+    def did(x):
+        latest[:] = [x]
+        return x
+
+    class Chunk:
+        def __init__(self, hi, lo):
+            self.hi, self.lo = hi, lo
+
+        def exchange_hi(self):
+            self.hi = go(self.hi)
+            self.hi_sib = swap("fsdp", 1, self.hi)
+
+        def exchange_lo(self):
+            self.lo = go(self.lo)
+            self.lo_sib = swap("fsdp", 1, self.lo)
+
+        def give(self):
+            hi = go(self.hi, self.hi_sib)
+            products = in_products(
+                core_arg, hi, lambda c: c, hi, lambda c: 2, weights, quarter, scale
+            )
+            self.got = by_core(FIRST, did(products.astype(f16)))
+
+        def keep(self):
+            hi, lo = go(self.hi, self.hi_sib), (self.lo, self.lo_sib)
+            self.kept = did(
+                in_products(core_arg, lo, lambda c: 0, hi, lambda c: 1 - c, weights, quarter, scale)
+            )
+
+        def second(self):
+            got, kept = go(self.got, self.kept)
+            give = did((kept[:, quarter:] + got[:, quarter:].astype(f32)).astype(f16))
+            self.kept = kept[:, :quarter] + got[:, :quarter].astype(f32)
+            self.got = by_core(SECOND, give)
+
+        def hidden(self):
+            got, kept = go(self.got, self.kept)
+            summed = (kept + got.astype(f32)) * (1.0 / scale)
+            self.own = did((jax.nn.silu(summed[0]) * summed[1]).astype(bf16))
+            self.got = by_core(SECOND, self.own)
+
+        def gather_half(self):
+            own, got = go(self.own, self.got)
+            self.own = did(jnp.concatenate([own, got], axis=0))
+            self.got = by_core(FIRST, self.own)
+            self.own_sib = swap("fsdp", 1, self.own)
+
+        def gather_whole(self):
+            self.got = did(go(self.got))
+            self.got_sib = swap("fsdp", 1, self.got)
+
+        def down(self, frozen_part):
+            own, got, own_sib, got_sib = go(self.own, self.got, self.own_sib, self.got_sib)
+
+            def rows_of(want):
+                def pick_rows(o, g, is_even):
+                    low = jnp.concatenate([o[:quarter], jnp.where(is_even, g[:quarter], o[quarter:])], axis=0)
+                    high = jnp.concatenate([jnp.where(is_even, o[quarter:], g[:quarter]), g[quarter:]], axis=0)
+                    return jnp.where(want, low, high)
+
+                mine = pick_rows(own, got, even)
+                theirs = pick_rows(own_sib, got_sib, jnp.logical_not(even))
+                return jnp.concatenate(
+                    [jnp.where(even, mine, theirs), jnp.where(even, theirs, mine)], axis=1
+                )
+
+            def mlp(rows_in):
+                return dot(rows_in, down_learn) - frozen_part * dot(rows_in, down_frozen)
+
+            other_rows = rows_of(jnp.logical_not(low_half))
+            own_rows_in = rows_of(low_half)
+            give = did(mlp(other_rows).astype(bf16))
+            self.got = swap("tensor", 1, give)
+            self.mlp = did(mlp(go(own_rows_in)))
+            self.parts = [own_rows_in, other_rows]
+
+        def pair(self):
+            mlp, got = go(self.mlp, self.got)
+            give = did((mlp + got.astype(f32)).astype(bf16))
+            self.far = swap("tensor", 3, give)
+
+        def delta(self, far):
+            mlp, got, far = go(self.mlp, self.got, far)
+            mlp = mlp + got.astype(f32) + far.astype(f32)
+            x = jnp.concatenate([self.lo, self.hi], axis=0)
+            base = jnp.where(low_half, x[:own_rows], x[own_rows:]).astype(f32)
+            diff = jnp.where(forget_first, mlp, base + mlp - target[None, :])
+            self.loss = jnp.sum(diff * diff)
+            mine = did((diff * jnp.where(forget_first, 2.0, 1.0)).astype(bf16))
+            self.back = swap("tensor", 3, mine)
+            self.delta_b = [mine, swap("tensor", 1, mine)]
+
+        def turn_back(self):
+            back = go(self.back)
+            self.delta_a = [back, swap("tensor", 1, back)]
+
+    mean_square = jnp.mean(steer * steer)
+    target_scale = 20.0 / jnp.sqrt(total * (mean_square + 1e-06))
+    target = target_scale * lax.dynamic_slice_in_dim(steer, me_f * cols, cols)
+
+    a, b = Chunk(hi_a, lo_a), Chunk(hi_b, lo_b)
+    a.exchange_hi()
+    a.exchange_lo()
+    a.give()
+    b.exchange_hi()
+    a.keep()
+    a.second()
+    b.give()
+    b.exchange_lo()
+    a.hidden()
+    a.gather_half()
+    b.keep()
+    a.gather_whole()
+    b.second()
+    a.down(frozen_a)
+    b.hidden()
+    b.gather_half()
+    a.pair()
+    b.gather_whole()
+    b.down(frozen_b)
+    b.delta(a.far)
+    value = jnp.full((8, 128), b.loss, f32)
+    value = did(value + go(swap("fsdp", 2, value)))
+    b.turn_back()
+    value = did(value + go(swap("fsdp", 4, value)))
+    value = did(value + go(swap("fsdp", 1, value)))
+    value = did(value + go(swap("tensor", 1, value)))
+    other = swap("tensor", 3, value)
+    hidden = did(turned(list(go(*a.parts, *b.parts))))
+    delta = jnp.concatenate(b.delta_a + b.delta_b, axis=0)
+    grad_down = did(dot(go(hidden), delta))
+    other = go(other)
+    sum_steer = jnp.where(forget_first, other, value)[0, 0]
+    sum_keep = jnp.where(forget_first, value, other)[0, 0]
+    count_f = jnp.sum(sample_lengths[0]).astype(f32)
+    count_r = jnp.sum(sample_lengths[1]).astype(f32)
+    losses = jnp.stack([sum_steer / (count_f * total), sum_keep / (count_r * total)])
+    return grad_down, losses
+
+
+def gathered_shards(tokens, gate_weight, up_weight, down_frozen, down_learn, steer, sample_lengths):
     rows_tp = tokens.shape[0]
     cols = tokens.shape[1]
     width_ff = gate_weight.shape[1]
@@ -78,8 +357,9 @@
 
 
 def solution(mesh):
+    paired = mesh.shape["fsdp"] == 8 and mesh.shape["tensor"] == 4
     return jax.shard_map(
-        shards,
+        paired_shards if paired else gathered_shards,
         mesh=mesh,
         in_specs=(
             P("tensor", "fsdp"),

time: 422 us -> 193 us (0.46)
  waiting for transfers between devices: 298 us -> 55.3 us
  starting transfers between devices: 0.38 us -> 49.2 us
  blocking collectives: 42.2 us -> 0 us
  Pallas kernels: 0 us -> 29.8 us
  matrix products: 44.2 us -> 25.2 us
  between operations: 16.9 us -> 4.54 us
  local copies, waits for them, and re-layouts: 7 us -> 11.7 us
  other arithmetic: 12.6 us -> 17 us
    reduce_scatter x2 -> x0, waiting for transfers between devices: 214 us -> none  [the longest x1 122 us: shards(): lax.psum_scatter(jnp.dot(block, both_in, preferred_element_type=jnp.float...]
    all_gather x3 -> x0, waiting for transfers between devices: 83.6 us -> none  [the longest x1 45.1 us: shards(): gathered = lax.all_gather(tokens, 'tensor', axis=0, tiled=True)]
    ppermute x0 -> x32, waiting for transfers between devices: none -> 55.3 us  [the longest x24 43.1 us: swap(): lax.ppermute(x, axis, [(i, i ^ bit) for i in range(lax.axis_size(axis))])]
    ppermute x0 -> x32, starting transfers between devices: none -> 49.2 us  [the longest x24 38.5 us: swap(): lax.ppermute(x, axis, [(i, i ^ bit) for i in range(lax.axis_size(axis))])]
    psum x1 -> x0, blocking collectives: 42.2 us -> none  [shards(): lax.psum((local_steer, local_keep), ('fsdp', 'tensor'))]
    pallas_call x0 -> x5, Pallas kernels: none -> 29.8 us  [the longest x4 27.9 us: in_products(): pl.pallas_call(lambda *refs: in_kernel(*refs, scale=scale), grid_spec=plt...]
    dot_general x3 -> x11, matrix products: 44.2 us -> 25.2 us  [dot(): return jnp.dot(a, b, preferred_element_type=f32)]
    dynamic_slice x0 -> x2, local copies, waits for them, and re-layouts: none -> 6.44 us  [given(): return lax.dynamic_slice_in_dim(w, (1 - core) * half, half, 1)]
  transfers between devices with their start and end apart: 5 -> 32, of which waited for: 4 -> 15; matrix products, arithmetic and copies ran while one was open for 2% -> 20% of each run, Pallas kernels for 0% -> 12%
where the time goes in v1:
time: 193 us
  waiting for transfers between devices  55.3 us (29%)
  starting transfers between devices  49.2 us (25%)
  Pallas kernels  29.8 us (15%)
  matrix products  25.2 us (13%)
  other arithmetic  17 us (9%)
  local copies, waits for them, and re-layouts  11.7 us (6%)
  between operations  4.54 us (2%)
    ppermute x24, waiting for transfers between devices, swap(): lax.ppermute(x, axis, [(i, i ^ bit) for i in range(lax.axis_size(axis))])  43.1 us
    ppermute x24, starting transfers between devices, swap(): lax.ppermute(x, axis, [(i, i ^ bit) for i in range(lax.axis_size(axis))])  38.5 us
    pallas_call x4, Pallas kernels, in_products(): pl.pallas_call(lambda *refs: in_kernel(*refs, scale=scale), grid_spec=plt...  27.9 us
    dot_general x11, matrix products, dot(): return jnp.dot(a, b, preferred_element_type=f32)  25.2 us
    ppermute x8, waiting for transfers between devices, by_core(): lax.ppermute(x, 'fsdp', [(i, i ^ (odd if i % 2 else even)) for i in range...  12.2 us
    ppermute x8, starting transfers between devices, by_core(): lax.ppermute(x, 'fsdp', [(i, i ^ (odd if i % 2 else even)) for i in range...  10.7 us
    dynamic_slice x2, local copies, waits for them, and re-layouts, given(): return lax.dynamic_slice_in_dim(w, (1 - core) * half, half, 1)  6.44 us
    select_n x4, other arithmetic, pick_rows(): jnp.where(is_even, g[:quarter], o[quarter:])  4.25 us
  transfers between devices with their start and end apart: 32, of which 15 were waited for; matrix products, arithmetic and copies ran while one was open for 20% of the time, Pallas kernels for 12%

profile of v1, /device:TPU:0, one launch (start us, length us, event | category | flops | bytes accessed | tf_op | source)
XLA Modules:
  0.0 192.9 jit_solution(11256917143975084530)
XLA Ops:
  0.7 4.3 %constant_dynamic-slice_fusion.1 = bf16[1024,1792]{1,0:T(8,128)(2,1)} fusion(bf16[1024,3584]{1,0:T(8,128)(2,1)} %refs_5_.7, s32[]{:T(128)S(6)} %select_n.302), kind=kLoop, calls=%fused_computation.134 | loop fusion | bytes 7340036 | tf_op jit(solution)/shard_map/dynamic_slice | solution.py:118
  6.2 2.1 %constant_dynamic-slice_fusion = bf16[1024,1792]{1,0:T(8,128)(2,1)} fusion(bf16[1024,3584]{1,0:T(8,128)(2,1)S(1)} %copy-done, s32[]{:T(128)S(6)} %select_n.302), kind=kLoop, calls=%fused_computation.133 | loop fusion | bytes 7340036 | tf_op jit(solution)/shard_map/dynamic_slice | solution.py:118
  8.8 3.0 %collective-permute-start = (bf16[256,1024]{1,0:T(8,128)(2,1)S(1)}, bf16[256,1024]{1,0:T(8,128)(2,1)S(1)}, u32[]{:S(2)}, u32[]{:S(2)}) collective-permute-start(bf16[256,1024]{1,0:T(8,128)(2,1)S(1)} %copy-done.6), channel_id=1, source_target_pairs={{0,1},{1,0},{2,3},{3,2},{4,5},{5,4},{6,7},{7,6},{8,9},{9,8},{10,11... | collective-permute-start | bytes 1572872 | tf_op jit(solution)/shard_map/ppermute | solution.py:34
  13.3 10.7 %collective-permute-done = bf16[256,1024]{1,0:T(8,128)(2,1)S(1)} collective-permute-done((bf16[256,1024]{1,0:T(8,128)(2,1)S(1)}, bf16[256,1024]{1,0:T(8,128)(2,1)S(1)}, u32[]{:S(2)}, u32[]{:S(2)}) %collective-permute-start) | collective-permute-done | bytes 524320 | tf_op jit(solution)/shard_map/ppermute | solution.py:34
  24.4 1.9 collective-permute-done.1.refs_3_.refs_4_
  26.3 6.9 %in_products.4 = f32[2,160,1792]{2,1,0:T(8,128)S(1)} custom-call(s32[1]{0:T(128)} %bitcast.refs_0_, bf16[240,1024]{1,0:T(8,128)(2,1)S(1)} %slice.178.refs_1_.refs_2_, bf16[240,1024]{1,0:T(8,128)(2,1)S(1)} %slice.178.refs_1_.refs_2_, bf16[240,1024]{1,0:T(8,128)(2,1)S(1)} %collective-permute-done.1.refs_3_.refs_4_, ...), custom_call_target="tpu_custom_call" | custom-call | tf_op jit(solution)/shard_map/in_products/pallas_call | solution.py:63
  33.4 1.7 collective-permute-start.4
  35.2 3.7 %collective-permute-start.7 = (bf16[240,1024]{1,0:T(8,128)(2,1)S(1)}, bf16[240,1024]{1,0:T(8,128)(2,1)S(1)}, u32[]{:S(2)}, u32[]{:S(2)}) collective-permute-start(bf16[240,1024]{1,0:T(8,128)(2,1)S(1)} %slice.178.refs_1_.refs_2_), channel_id=1, source_target_pairs={{0,3},{1,2},{2,1},{3,0},{4,7},{5,6},{6,5},{7,4},{8,11},{9,10},{10,... | collective-permute-start | bytes 1474568 | tf_op jit(solution)/shard_map/ppermute | solution.py:34
  38.8 6.9 %in_products.5 = f32[2,160,1792]{2,1,0:T(8,128)S(1)} custom-call(s32[1]{0:T(128)} %bitcast.refs_0_, bf16[80,1024]{1,0:T(8,128)(2,1)S(1)} %slice.179.refs_1_, bf16[240,1024]{1,0:T(8,128)(2,1)S(1)} %slice.178.refs_1_.refs_2_, bf16[80,1024]{1,0:T(8,128)(2,1)S(1)} %collective-permute-done.5.refs_3_, ...), custom_call_target="tpu_custom_call" | custom-call | tf_op jit(solution)/shard_map/in_products/pallas_call | solution.py:63
  45.8 3.5 %collective-permute-done.4 = f16[2,160,1792]{2,1,0:T(8,128)(2,1)S(1)} collective-permute-done((f16[2,160,1792]{2,1,0:T(8,128)(2,1)S(1)}, f16[2,160,1792]{2,1,0:T(8,128)(2,1)S(1)}, u32[]{:S(2)}, u32[]{:S(2)}) %collective-permute-start.4) | collective-permute-done | bytes 1146912 | tf_op jit(solution)/shard_map/ppermute | solution.py:40
  49.5 1.8 collective-permute-start.6
  51.3 1.9 collective-permute-done.8.refs_3_.refs_4_
  53.1 6.9 %in_products.6 = f32[2,160,1792]{2,1,0:T(8,128)S(1)} custom-call(s32[1]{0:T(128)} %bitcast.refs_0_, bf16[240,1024]{1,0:T(8,128)(2,1)S(1)} %collective-permute-done.7.refs_1_.refs_2_, bf16[240,1024]{1,0:T(8,128)(2,1)S(1)} %collective-permute-done.7.refs_1_.refs_2_, bf16[240,1024]{1,0:T(8,128)(2,1)S(1)} %collective-permute-done.8.refs_3_.refs_4_, ...), custom_call_target="tpu_custom_call" | custom-call | tf_op jit(solution)/shard_map/in_products/pallas_call | solution.py:63
  63.5 7.2 %collective-permute-done.9 = bf16[80,1792]{1,0:T(8,128)(2,1)S(1)} collective-permute-done((bf16[80,1792]{1,0:T(8,128)(2,1)S(1)}, bf16[80,1792]{1,0:T(8,128)(2,1)S(1)}, u32[]{:S(2)}, u32[]{:S(2)}) %collective-permute-start.9) | collective-permute-done | bytes 286752 | tf_op jit(solution)/shard_map/ppermute | solution.py:40
  70.8 2.0 %collective-permute-start.10 = (bf16[160,1792]{1,0:T(8,128)(2,1)S(1)}, bf16[160,1792]{1,0:T(8,128)(2,1)}, u32[]{:S(2)}, u32[]{:S(2)}) collective-permute-start(bf16[160,1792]{1,0:T(8,128)(2,1)S(1)} %constant_dynamic-update-slice_fusion), channel_id=1, source_target_pairs={{0,8},{4,20},{8,0},{12,28},{16,24},{20,4},{24,16},{28,12},{1,9},{5... | collective-permute-start | bytes 1720328 | tf_op jit(solution)/shard_map/ppermute | solution.py:40
  72.8 3.6 %collective-permute-start.11 = (bf16[80,1024]{1,0:T(8,128)(2,1)S(1)}, bf16[80,1024]{1,0:T(8,128)(2,1)S(1)}, u32[]{:S(2)}, u32[]{:S(2)}) collective-permute-start(bf16[80,1024]{1,0:T(8,128)(2,1)S(1)} %slice.179.refs_1_), channel_id=1, source_target_pairs={{0,3},{1,2},{2,1},{3,0},{4,7},{5,6},{6,5},{7,4},{8,11},{9,10},{10,... | collective-permute-start | bytes 491528 | tf_op jit(solution)/shard_map/ppermute | solution.py:34
  76.4 3.5 %collective-permute-done.11.refs_1_ = bf16[80,1024]{1,0:T(8,128)(2,1)S(1)} collective-permute-done((bf16[80,1024]{1,0:T(8,128)(2,1)S(1)}, bf16[80,1024]{1,0:T(8,128)(2,1)S(1)}, u32[]{:S(2)}, u32[]{:S(2)}) %collective-permute-start.11) | collective-permute-done | bytes 163872 | tf_op jit(solution)/shard_map/ppermute | solution.py:34
  81.5 7.1 %in_products.7 = f32[2,160,1792]{2,1,0:T(8,128)S(1)} custom-call(s32[1]{0:T(128)} %bitcast.refs_0_, bf16[80,1024]{1,0:T(8,128)(2,1)S(1)} %collective-permute-done.11.refs_1_, bf16[240,1024]{1,0:T(8,128)(2,1)S(1)} %collective-permute-done.7.refs_1_.refs_2_, bf16[80,1024]{1,0:T(8,128)(2,1)S(1)} %collective-permute-done.12.refs_3_, ...), custom_call_target="tpu_custom_call" | custom-call | tf_op jit(solution)/shard_map/in_products/pallas_call | solution.py:63
  104.3 7.4 %collective-permute-start.19 = (bf16[160,1024]{1,0:T(8,128)(2,1)S(1)}, bf16[160,1024]{1,0:T(8,128)(2,1)S(1)}, u32[]{:S(2)}, u32[]{:S(2)}) collective-permute-start(bf16[160,1024]{1,0:T(8,128)(2,1)S(1)} %fusion.14), channel_id=1, source_target_pairs={{0,1},{1,0},{2,3},{3,2},{4,5},{5,4},{6,7},{7,6},{8,9},{9,8},{10,11... | collective-permute-start | bytes 983048 | tf_op jit(solution)/shard_map/ppermute | solution.py:34
  112.9 6.2 %collective-permute-done.19 = bf16[160,1024]{1,0:T(8,128)(2,1)S(1)} collective-permute-done((bf16[160,1024]{1,0:T(8,128)(2,1)S(1)}, bf16[160,1024]{1,0:T(8,128)(2,1)S(1)}, u32[]{:S(2)}, u32[]{:S(2)}) %collective-permute-start.19) | collective-permute-done | bytes 327712 | tf_op jit(solution)/shard_map/ppermute | solution.py:34
  122.8 2.5 %collective-permute-start.23 = (bf16[160,1024]{1,0:T(8,128)(2,1)}, bf16[160,1024]{1,0:T(8,128)(2,1)S(1)}, u32[]{:S(2)}, u32[]{:S(2)}) collective-permute-start(bf16[160,1024]{1,0:T(8,128)(2,1)} %add_convert_fusion.2), channel_id=1, source_target_pairs={{0,3},{1,2},{2,1},{3,0},{4,7},{5,6},{6,5},{7,4},{8,11},{9,10},{10,... | collective-permute-start | bytes 983048 | tf_op jit(solution)/shard_map/ppermute | solution.py:34
  127.8 5.1 %fusion.40 = f32[160,1024]{1,0:T(8,128)S(1)} fusion(bf16[3584,1024]{1,0:T(8,128)(2,1)} %param.11, bf16[160,1792]{1,0:T(8,128)(2,1)S(1)} %get-tuple-element.122, bf16[160,1792]{1,0:T(8,128)(2,1)S(1)} %get-tuple-element.120), kind=kOutput, calls=%fused_computation.138 | convolution fusion | flops 1176698880 | bytes 9142272 | tf_op jit(solution)/shard_map/dot_general | solution.py:30
  134.4 4.9 %collective-permute-start.22 = (bf16[160,1024]{1,0:T(8,128)(2,1)S(1)}, bf16[160,1024]{1,0:T(8,128)(2,1)S(1)}, u32[]{:S(2)}, u32[]{:S(2)}) collective-permute-start(bf16[160,1024]{1,0:T(8,128)(2,1)S(1)} %fusion.13), channel_id=1, source_target_pairs={{0,1},{1,0},{2,3},{3,2},{4,5},{5,4},{6,7},{7,6},{8,9},{9,8},{10,11... | collective-permute-start | bytes 983048 | tf_op jit(solution)/shard_map/ppermute | solution.py:34
  139.4 1.7 fusion.43
  142.5 4.8 %collective-permute-done.22 = bf16[160,1024]{1,0:T(8,128)(2,1)S(1)} collective-permute-done((bf16[160,1024]{1,0:T(8,128)(2,1)S(1)}, bf16[160,1024]{1,0:T(8,128)(2,1)S(1)}, u32[]{:S(2)}, u32[]{:S(2)}) %collective-permute-start.22) | collective-permute-done | bytes 327712 | tf_op jit(solution)/shard_map/ppermute | solution.py:34
  151.3 2.2 %collective-permute-done.24 = f32[8,128]{1,0:T(8,128)S(1)} collective-permute-done((f32[8,128]{1,0:T(8,128)S(1)}, f32[8,128]{1,0:T(8,128)S(1)}, u32[]{:S(2)}, u32[]{:S(2)}) %collective-permute-start.24) | collective-permute-done | bytes 4128 | tf_op jit(solution)/shard_map/ppermute | solution.py:34
  160.0 1.6 collective-permute-start.30
  162.1 6.5 %collective-permute-done.28 = bf16[160,1024]{1,0:T(8,128)(2,1)S(1)} collective-permute-done((bf16[160,1024]{1,0:T(8,128)(2,1)}, bf16[160,1024]{1,0:T(8,128)(2,1)S(1)}, u32[]{:S(2)}, u32[]{:S(2)}) %collective-permute-start.28) | collective-permute-done | bytes 327712 | tf_op jit(solution)/shard_map/ppermute | solution.py:34
  168.6 4.4 %collective-permute-start.29 = (bf16[160,1024]{1,0:T(8,128)(2,1)S(1)}, bf16[160,1024]{1,0:T(8,128)(2,1)S(1)}, u32[]{:S(2)}, u32[]{:S(2)}) collective-permute-start(bf16[160,1024]{1,0:T(8,128)(2,1)S(1)} %collective-permute-done.28), channel_id=1, source_target_pairs={{0,1},{1,0},{2,3},{3,2},{4,5},{5,4},{6,7},{7,6},{8,9},{9,8},{10,11... | collective-permute-start | bytes 983048 | tf_op jit(solution)/shard_map/ppermute | solution.py:34
  175.1 2.0 %turned.1 = bf16[3584,640]{1,0:T(8,128)(2,1)S(1)} custom-call(bf16[160,3584]{1,0:T(8,128)(2,1)S(1)} %pad_maximum_fusion.refs_0_, bf16[160,3584]{1,0:T(8,128)(2,1)S(1)} %pad_maximum_fusion.1.refs_1_, bf16[160,3584]{1,0:T(8,128)(2,1)S(1)} %pad_maximum_fusion.2.refs_2_, bf16[160,3584]{1,0:T(8,128)(2,1)S(1)} %pad_maximum_fusion.3.refs_3_), custom_call_target="tpu_custom_call" | custom-call | tf_op jit(solution)/shard_map/turned/pallas_call | solution.py:86
  177.1 3.6 %collective-permute-done.29 = bf16[160,1024]{1,0:T(8,128)(2,1)S(1)} collective-permute-done((bf16[160,1024]{1,0:T(8,128)(2,1)S(1)}, bf16[160,1024]{1,0:T(8,128)(2,1)S(1)}, u32[]{:S(2)}, u32[]{:S(2)}) %collective-permute-start.29) | collective-permute-done | bytes 327712 | tf_op jit(solution)/shard_map/ppermute | solution.py:34
  180.7 9.2 %fusion.1 = f32[3584,1024]{1,0:T(8,128)} fusion(bf16[3584,640]{1,0:T(8,128)(2,1)S(1)} %turned.1, bf16[160,1024]{1,0:T(8,128)(2,1)S(1)} %collective-permute-done.30, bf16[160,1024]{1,0:T(8,128)(2,1)S(1)} %copy-done.7, bf16[160,1024]{1,0:T(8,128)(2,1)S(1)} %collective-permute-done.29, bf16[160,1024]{1,0:T(8,128)(2,1)S(1)} %collective-permute-done.28), kind=kOutput, calls=%fused_computation.2 | convolution fusion | flops 4702863360 | bytes 20578304 | tf_op jit(solution)/shard_map/dot_general | solution.py:30
  (138 shorter events, 47.5 us)
Async XLA Ops:
  8.3 18.0 %collective-permute-start.3 = (bf16[1024,1792]{1,0:T(8,128)(2,1)}, bf16[1024,1792]{1,0:T(8,128)(2,1)}, u32[]{:S(2)}, u32[]{:S(2)}) collective-permute-start(bf16[1024,1792]{1,0:T(8,128)(2,1)} %constant_dynamic-slice_fusion), channel_id=1, source_target_pairs={{0,4},{4,0},{8,12},{12,8},{16,20},{20,16},{24,28},{28,24},{1,5},{5... | collective-permute-start | bytes 11010056 | tf_op jit(solution)/shard_map/ppermute | solution.py:34
  8.8 17.5 %collective-permute-start.2 = (bf16[1024,1792]{1,0:T(8,128)(2,1)}, bf16[1024,1792]{1,0:T(8,128)(2,1)}, u32[]{:S(2)}, u32[]{:S(2)}) collective-permute-start(bf16[1024,1792]{1,0:T(8,128)(2,1)} %constant_dynamic-slice_fusion.1), channel_id=1, source_target_pairs={{0,4},{4,0},{8,12},{12,8},{16,20},{20,16},{24,28},{28,24},{1,5},{5... | collective-permute-start | bytes 11010056 | tf_op jit(solution)/shard_map/ppermute | solution.py:34
  8.8 15.1 %collective-permute-start = (bf16[256,1024]{1,0:T(8,128)(2,1)S(1)}, bf16[256,1024]{1,0:T(8,128)(2,1)S(1)}, u32[]{:S(2)}, u32[]{:S(2)}) collective-permute-start(bf16[256,1024]{1,0:T(8,128)(2,1)S(1)} %copy-done.6), channel_id=1, source_target_pairs={{0,1},{1,0},{2,3},{3,2},{4,5},{5,4},{6,7},{7,6},{8,9},{9,8},{10,11... | collective-permute-start | bytes 1572872 | tf_op jit(solution)/shard_map/ppermute | solution.py:34
  24.4 1.9 %collective-permute-start.1 = (bf16[240,1024]{1,0:T(8,128)(2,1)S(1)}, bf16[240,1024]{1,0:T(8,128)(2,1)S(1)}, u32[]{:S(2)}, u32[]{:S(2)}) collective-permute-start(bf16[240,1024]{1,0:T(8,128)(2,1)S(1)} %slice.178.refs_1_.refs_2_), channel_id=1, source_target_pairs={{0,4},{4,0},{8,12},{12,8},{16,20},{20,16},{24,28},{28,24},{1,5},{5... | collective-permute-start | bytes 1474568 | tf_op jit(solution)/shard_map/ppermute | solution.py:34
  33.4 15.9 %collective-permute-start.4 = (f16[2,160,1792]{2,1,0:T(8,128)(2,1)S(1)}, f16[2,160,1792]{2,1,0:T(8,128)(2,1)S(1)}, u32[]{:S(2)}, u32[]{:S(2)}) collective-permute-start(f16[2,160,1792]{2,1,0:T(8,128)(2,1)S(1)} %convert_element_type.72), channel_id=1, source_target_pairs={{0,8},{4,20},{8,0},{12,28},{16,24},{20,4},{24,16},{28,12},{1,9},{5... | collective-permute-start | bytes 3440648 | tf_op jit(solution)/shard_map/ppermute | solution.py:40
  35.1 3.7 %collective-permute-start.5 = (bf16[80,1024]{1,0:T(8,128)(2,1)S(1)}, bf16[80,1024]{1,0:T(8,128)(2,1)S(1)}, u32[]{:S(2)}, u32[]{:S(2)}) collective-permute-start(bf16[80,1024]{1,0:T(8,128)(2,1)S(1)} %slice.179.refs_1_), channel_id=1, source_target_pairs={{0,4},{4,0},{8,12},{12,8},{16,20},{20,16},{24,28},{28,24},{1,5},{5... | collective-permute-start | bytes 491528 | tf_op jit(solution)/shard_map/ppermute | solution.py:34
  35.2 16.1 %collective-permute-start.7 = (bf16[240,1024]{1,0:T(8,128)(2,1)S(1)}, bf16[240,1024]{1,0:T(8,128)(2,1)S(1)}, u32[]{:S(2)}, u32[]{:S(2)}) collective-permute-start(bf16[240,1024]{1,0:T(8,128)(2,1)S(1)} %slice.178.refs_1_.refs_2_), channel_id=1, source_target_pairs={{0,3},{1,2},{2,1},{3,0},{4,7},{5,6},{6,5},{7,4},{8,11},{9,10},{10,... | collective-permute-start | bytes 1474568 | tf_op jit(solution)/shard_map/ppermute | solution.py:34
  49.5 11.7 %collective-permute-start.6 = (f16[2,80,1792]{2,1,0:T(8,128)(2,1)S(1)}, f16[2,80,1792]{2,1,0:T(8,128)(2,1)S(1)}, u32[]{:S(2)}, u32[]{:S(2)}) collective-permute-start(f16[2,80,1792]{2,1,0:T(8,128)(2,1)S(1)} %get-tuple-element.119), channel_id=1, source_target_pairs={{0,16},{4,12},{8,24},{12,4},{16,0},{20,28},{24,8},{28,20},{1,17},{... | collective-permute-start | bytes 1720328 | tf_op jit(solution)/shard_map/ppermute | solution.py:40
  51.3 1.9 collective-permute-start.8
  61.5 9.2 %collective-permute-start.9 = (bf16[80,1792]{1,0:T(8,128)(2,1)S(1)}, bf16[80,1792]{1,0:T(8,128)(2,1)S(1)}, u32[]{:S(2)}, u32[]{:S(2)}) collective-permute-start(bf16[80,1792]{1,0:T(8,128)(2,1)S(1)} %fusion.18), channel_id=1, source_target_pairs={{0,16},{4,12},{8,24},{12,4},{16,0},{20,28},{24,8},{28,20},{1,17},{... | collective-permute-start | bytes 860168 | tf_op jit(solution)/shard_map/ppermute | solution.py:40
  62.6 26.3 %collective-permute-start.15 = (f16[2,160,1792]{2,1,0:T(8,128)(2,1)}, f16[2,160,1792]{2,1,0:T(8,128)(2,1)}, u32[]{:S(2)}, u32[]{:S(2)}) collective-permute-start(f16[2,160,1792]{2,1,0:T(8,128)(2,1)} %convert_element_type.76), channel_id=1, source_target_pairs={{0,8},{4,20},{8,0},{12,28},{16,24},{20,4},{24,16},{28,12},{1,9},{5... | collective-permute-start | bytes 3440648 | tf_op jit(solution)/shard_map/ppermute | solution.py:40
  70.8 17.8 %collective-permute-start.10 = (bf16[160,1792]{1,0:T(8,128)(2,1)S(1)}, bf16[160,1792]{1,0:T(8,128)(2,1)}, u32[]{:S(2)}, u32[]{:S(2)}) collective-permute-start(bf16[160,1792]{1,0:T(8,128)(2,1)S(1)} %constant_dynamic-update-slice_fusion), channel_id=1, source_target_pairs={{0,8},{4,20},{8,0},{12,28},{16,24},{20,4},{24,16},{28,12},{1,9},{5... | collective-permute-start | bytes 1720328 | tf_op jit(solution)/shard_map/ppermute | solution.py:40
  72.8 7.1 %collective-permute-start.11 = (bf16[80,1024]{1,0:T(8,128)(2,1)S(1)}, bf16[80,1024]{1,0:T(8,128)(2,1)S(1)}, u32[]{:S(2)}, u32[]{:S(2)}) collective-permute-start(bf16[80,1024]{1,0:T(8,128)(2,1)S(1)} %slice.179.refs_1_), channel_id=1, source_target_pairs={{0,3},{1,2},{2,1},{3,0},{4,7},{5,6},{6,5},{7,4},{8,11},{9,10},{10,... | collective-permute-start | bytes 491528 | tf_op jit(solution)/shard_map/ppermute | solution.py:34
  79.9 1.6 collective-permute-start.12
  79.9 10.8 %collective-permute-start.13 = (bf16[160,1792]{1,0:T(8,128)(2,1)S(1)}, bf16[160,1792]{1,0:T(8,128)(2,1)}, u32[]{:S(2)}, u32[]{:S(2)}) collective-permute-start(bf16[160,1792]{1,0:T(8,128)(2,1)S(1)} %constant_dynamic-update-slice_fusion), channel_id=1, source_target_pairs={{0,4},{4,0},{8,12},{12,8},{16,20},{20,16},{24,28},{28,24},{1,5},{5... | collective-permute-start | bytes 1720328 | tf_op jit(solution)/shard_map/ppermute | solution.py:34
  88.6 2.4 %collective-permute-start.14 = (bf16[160,1792]{1,0:T(8,128)(2,1)}, bf16[160,1792]{1,0:T(8,128)(2,1)}, u32[]{:S(2)}, u32[]{:S(2)}) collective-permute-start(bf16[160,1792]{1,0:T(8,128)(2,1)} %collective-permute-done.10), channel_id=1, source_target_pairs={{0,4},{4,0},{8,12},{12,8},{16,20},{20,16},{24,28},{28,24},{1,5},{5... | collective-permute-start | bytes 1720328 | tf_op jit(solution)/shard_map/ppermute | solution.py:34
  90.3 12.2 %collective-permute-start.16 = (f16[2,80,1792]{2,1,0:T(8,128)(2,1)S(1)}, f16[2,80,1792]{2,1,0:T(8,128)(2,1)S(1)}, u32[]{:S(2)}, u32[]{:S(2)}) collective-permute-start(f16[2,80,1792]{2,1,0:T(8,128)(2,1)S(1)} %get-tuple-element.117), channel_id=1, source_target_pairs={{0,16},{4,12},{8,24},{12,4},{16,0},{20,28},{24,8},{28,20},{1,17},{... | collective-permute-start | bytes 1720328 | tf_op jit(solution)/shard_map/ppermute | solution.py:40
  102.8 8.8 %collective-permute-start.17 = (bf16[80,1792]{1,0:T(8,128)(2,1)S(1)}, bf16[80,1792]{1,0:T(8,128)(2,1)S(1)}, u32[]{:S(2)}, u32[]{:S(2)}) collective-permute-start(bf16[80,1792]{1,0:T(8,128)(2,1)S(1)} %fusion.16), channel_id=1, source_target_pairs={{0,16},{4,12},{8,24},{12,4},{16,0},{20,28},{24,8},{28,20},{1,17},{... | collective-permute-start | bytes 860168 | tf_op jit(solution)/shard_map/ppermute | solution.py:40
  104.3 14.9 %collective-permute-start.19 = (bf16[160,1024]{1,0:T(8,128)(2,1)S(1)}, bf16[160,1024]{1,0:T(8,128)(2,1)S(1)}, u32[]{:S(2)}, u32[]{:S(2)}) collective-permute-start(bf16[160,1024]{1,0:T(8,128)(2,1)S(1)} %fusion.14), channel_id=1, source_target_pairs={{0,1},{1,0},{2,3},{3,2},{4,5},{5,4},{6,7},{7,6},{8,9},{9,8},{10,11... | collective-permute-start | bytes 983048 | tf_op jit(solution)/shard_map/ppermute | solution.py:34
  111.7 9.8 %collective-permute-start.18 = (bf16[160,1792]{1,0:T(8,128)(2,1)S(1)}, bf16[160,1792]{1,0:T(8,128)(2,1)S(1)}, u32[]{:S(2)}, u32[]{:S(2)}) collective-permute-start(bf16[160,1792]{1,0:T(8,128)(2,1)S(1)} %constant_dynamic-update-slice_fusion.2), channel_id=1, source_target_pairs={{0,8},{4,20},{8,0},{12,28},{16,24},{20,4},{24,16},{28,12},{1,9},{5... | collective-permute-start | bytes 1720328 | tf_op jit(solution)/shard_map/ppermute | solution.py:40
  112.9 12.4 %collective-permute-start.20 = (bf16[160,1792]{1,0:T(8,128)(2,1)S(1)}, bf16[160,1792]{1,0:T(8,128)(2,1)}, u32[]{:S(2)}, u32[]{:S(2)}) collective-permute-start(bf16[160,1792]{1,0:T(8,128)(2,1)S(1)} %constant_dynamic-update-slice_fusion.2), channel_id=1, source_target_pairs={{0,4},{4,0},{8,12},{12,8},{16,20},{20,16},{24,28},{28,24},{1,5},{5... | collective-permute-start | bytes 1720328 | tf_op jit(solution)/shard_map/ppermute | solution.py:34
  121.5 3.9 %collective-permute-start.21 = (bf16[160,1792]{1,0:T(8,128)(2,1)S(1)}, bf16[160,1792]{1,0:T(8,128)(2,1)}, u32[]{:S(2)}, u32[]{:S(2)}) collective-permute-start(bf16[160,1792]{1,0:T(8,128)(2,1)S(1)} %collective-permute-done.18), channel_id=1, source_target_pairs={{0,4},{4,0},{8,12},{12,8},{16,20},{20,16},{24,28},{28,24},{1,5},{5... | collective-permute-start | bytes 1720328 | tf_op jit(solution)/shard_map/ppermute | solution.py:34
  122.8 19.7 %collective-permute-start.23 = (bf16[160,1024]{1,0:T(8,128)(2,1)}, bf16[160,1024]{1,0:T(8,128)(2,1)S(1)}, u32[]{:S(2)}, u32[]{:S(2)}) collective-permute-start(bf16[160,1024]{1,0:T(8,128)(2,1)} %add_convert_fusion.2), channel_id=1, source_target_pairs={{0,3},{1,2},{2,1},{3,0},{4,7},{5,6},{6,5},{7,4},{8,11},{9,10},{10,... | collective-permute-start | bytes 983048 | tf_op jit(solution)/shard_map/ppermute | solution.py:34
  134.4 13.0 %collective-permute-start.22 = (bf16[160,1024]{1,0:T(8,128)(2,1)S(1)}, bf16[160,1024]{1,0:T(8,128)(2,1)S(1)}, u32[]{:S(2)}, u32[]{:S(2)}) collective-permute-start(bf16[160,1024]{1,0:T(8,128)(2,1)S(1)} %fusion.13), channel_id=1, source_target_pairs={{0,1},{1,0},{2,3},{3,2},{4,5},{5,4},{6,7},{7,6},{8,9},{9,8},{10,11... | collective-permute-start | bytes 983048 | tf_op jit(solution)/shard_map/ppermute | solution.py:34
  149.8 3.7 %collective-permute-start.24 = (f32[8,128]{1,0:T(8,128)S(1)}, f32[8,128]{1,0:T(8,128)S(1)}, u32[]{:S(2)}, u32[]{:S(2)}) collective-permute-start(f32[8,128]{1,0:T(8,128)S(1)} %broadcast_in_dim.58), channel_id=1, source_target_pairs={{0,8},{4,12},{8,0},{12,4},{16,24},{20,28},{24,16},{28,20},{1,9},{5... | collective-permute-start | bytes 12296 | tf_op jit(solution)/shard_map/ppermute | solution.py:34
  154.1 3.9 %collective-permute-start.25 = (f32[8,128]{1,0:T(8,128)S(1)}, f32[8,128]{1,0:T(8,128)S(1)}, u32[]{:S(2)}, u32[]{:S(2)}) collective-permute-start(f32[8,128]{1,0:T(8,128)S(1)} %broadcast_add_fusion), channel_id=1, source_target_pairs={{0,16},{4,20},{8,24},{12,28},{16,0},{20,4},{24,8},{28,12},{1,17},{... | collective-permute-start | bytes 12296 | tf_op jit(solution)/shard_map/ppermute | solution.py:34
  156.4 12.2 %collective-permute-start.28 = (bf16[160,1024]{1,0:T(8,128)(2,1)}, bf16[160,1024]{1,0:T(8,128)(2,1)S(1)}, u32[]{:S(2)}, u32[]{:S(2)}) collective-permute-start(bf16[160,1024]{1,0:T(8,128)(2,1)} %get-tuple-element.114), channel_id=1, source_target_pairs={{0,3},{1,2},{2,1},{3,0},{4,7},{5,6},{6,5},{7,4},{8,11},{9,10},{10,... | collective-permute-start | bytes 983048 | tf_op jit(solution)/shard_map/ppermute | solution.py:34
  158.7 3.0 %collective-permute-start.26 = (f32[8,128]{1,0:T(8,128)S(1)}, f32[8,128]{1,0:T(8,128)S(1)}, u32[]{:S(2)}, u32[]{:S(2)}) collective-permute-start(f32[8,128]{1,0:T(8,128)S(1)} %fusion.59), channel_id=1, source_target_pairs={{0,4},{4,0},{8,12},{12,8},{16,20},{20,16},{24,28},{28,24},{1,5},{5... | collective-permute-start | bytes 12296 | tf_op jit(solution)/shard_map/ppermute | solution.py:34
  160.0 17.1 %collective-permute-start.30 = (bf16[160,1024]{1,0:T(8,128)(2,1)S(1)}, bf16[160,1024]{1,0:T(8,128)(2,1)S(1)}, u32[]{:S(2)}, u32[]{:S(2)}) collective-permute-start(bf16[160,1024]{1,0:T(8,128)(2,1)S(1)} %copy-done.7), channel_id=1, source_target_pairs={{0,1},{1,0},{2,3},{3,2},{4,5},{5,4},{6,7},{7,6},{8,9},{9,8},{10,11... | collective-permute-start | bytes 983048 | tf_op jit(solution)/shard_map/ppermute | solution.py:34
  161.6 12.0 %collective-permute-start.27 = (f32[8,128]{1,0:T(8,128)S(1)}, f32[8,128]{1,0:T(8,128)S(1)}, u32[]{:S(2)}, u32[]{:S(2)}) collective-permute-start(f32[8,128]{1,0:T(8,128)S(1)} %add.197), channel_id=1, source_target_pairs={{0,1},{1,0},{2,3},{3,2},{4,5},{5,4},{6,7},{7,6},{8,9},{9,8},{10,11... | collective-permute-start | bytes 12296 | tf_op jit(solution)/shard_map/ppermute | solution.py:34
  168.6 12.1 %collective-permute-start.29 = (bf16[160,1024]{1,0:T(8,128)(2,1)S(1)}, bf16[160,1024]{1,0:T(8,128)(2,1)S(1)}, u32[]{:S(2)}, u32[]{:S(2)}) collective-permute-start(bf16[160,1024]{1,0:T(8,128)(2,1)S(1)} %collective-permute-done.28), channel_id=1, source_target_pairs={{0,1},{1,0},{2,3},{3,2},{4,5},{5,4},{6,7},{7,6},{8,9},{9,8},{10,11... | collective-permute-start | bytes 983048 | tf_op jit(solution)/shard_map/ppermute | solution.py:34
  173.6 16.3 %collective-permute-start.31 = (f32[8,128]{1,0:T(8,128)S(1)}, f32[8,128]{1,0:T(8,128)S(1)}, u32[]{:S(2)}, u32[]{:S(2)}) collective-permute-start(f32[8,128]{1,0:T(8,128)S(1)} %add.198), channel_id=1, source_target_pairs={{0,3},{1,2},{2,1},{3,0},{4,7},{5,6},{6,5},{7,4},{8,11},{9,10},{10,... | collective-permute-start | bytes 12296 | tf_op jit(solution)/shard_map/ppermute | solution.py:34
  (18 other events, 118.2 us)

commit v2 on v1

--- a/solution.py
+++ b/solution.py
@@ -12,11 +12,13 @@
 TOKEN_BOUND = 6.0
 WEIGHT_BOUND = 0.0625
 HALF_MAX = 65504.0
-VMEM_BYTES = 8 * 1024 * 1024
+SIB_PARTS = 2
+GRAD_VMEM_BYTES = 56 * 1024 * 1024
 IN_VMEM_BYTES = 50 * 1024 * 1024
 f32 = jnp.float32
 bf16 = jnp.bfloat16
 f16 = jnp.float16
+FREE = pl.CostEstimate(flops=0, bytes_accessed=0, transcendentals=0)
 FIRST = (2, 4)
 SECOND = (4, 2)
 
@@ -44,54 +46,70 @@
     return lax.optimization_barrier((x,) + others)[0]
 
 
-def in_kernel(core_ref, x1_ref, x2_ref, s1_ref, s2_ref, wg_ref, wu_ref, sg_ref, su_ref, out_ref, *, scale):
+def in_kernel(core_ref, x1_ref, x2_ref, s1_ref, s2_ref, wg_ref, wu_ref, *refs, scale):
     x = jnp.concatenate([x1_ref[...], x2_ref[...]], axis=0)
     xs = jnp.concatenate([s1_ref[...], s2_ref[...]], axis=0)
-    out_ref[0] = (dot(x, wg_ref[...]) + dot(xs, sg_ref[...])) * scale
-    out_ref[1] = (dot(x, wu_ref[...]) + dot(xs, su_ref[...])) * scale
-
-
-def in_products(core, first, first_at, second, second_at, weights, quarter, scale):
+    *sibs, out_ref = refs
+    n = len(sibs) // 2
+    depth = x.shape[1] // n
+    for i, own_ref in enumerate((wg_ref, wu_ref)):
+        total = dot(x, own_ref[...])
+        for k, sib_ref in enumerate(sibs[i * n : (i + 1) * n]):
+            total += dot(xs[:, k * depth : (k + 1) * depth], sib_ref[...])
+        out_ref[i] = total * scale
+
+
+def in_products(core, x, x_sib, first_at, second_at, weights, quarter, scale, cost):
     gate_weight, up_weight, gate_sib, up_sib = weights
-    cols, half = gate_sib.shape
+    cols = x.shape[1]
+    depth, half = gate_sib[0].shape
     steps = 2
     tile = half // steps
     rows1 = pl.BlockSpec((quarter, cols), lambda j, c: (first_at(c[0]), 0))
     rows2 = pl.BlockSpec((quarter, cols), lambda j, c: (second_at(c[0]), 0))
     own = pl.BlockSpec((cols, tile), lambda j, c: (0, c[0] * steps + j))
-    sib = pl.BlockSpec((cols, tile), lambda j, c: (0, j))
+    sib = pl.BlockSpec((depth, tile), lambda j, c: (0, j))
     return pl.pallas_call(
         lambda *refs: in_kernel(*refs, scale=scale),
         grid_spec=pltpu.PrefetchScalarGridSpec(
             num_scalar_prefetch=1,
             grid=(steps,),
-            in_specs=[rows1, rows2, rows1, rows2, own, own, sib, sib],
+            in_specs=[rows1, rows2, rows1, rows2, own, own] + [sib] * (2 * len(gate_sib)),
             out_specs=pl.BlockSpec((2, 2 * quarter, tile), lambda j, c: (0, 0, j)),
         ),
         out_shape=jax.ShapeDtypeStruct((2, 2 * quarter, half), f32),
         compiler_params=pltpu.CompilerParams(vmem_limit_bytes=IN_VMEM_BYTES),
+        cost_estimate=cost,
         name="in_products",
-    )(core, first[0], second[0], first[1], second[1], gate_weight, up_weight, gate_sib, up_sib)
-
-
-def turn_kernel(*refs):
-    *parts, out_ref = refs
-    out_ref[...] = jnp.concatenate([p[...] for p in parts], axis=0).T
-
-
-def turned(parts):
-    width = parts[0].shape[1]
-    rows = sum(p.shape[0] for p in parts)
-    tile = 512
+    )(core, x, x, x_sib, x_sib, gate_weight, up_weight, *gate_sib, *up_sib)
+
+
+def grad_kernel(*refs):
+    *operands, out_ref = refs
+    n = len(operands) // 2
+    hidden = jnp.concatenate([h[...] for h in operands[:n]], axis=0)
+    delta = jnp.concatenate([d[...] for d in operands[n:]], axis=0)
+    out_ref[...] = lax.dot_general(
+        hidden, delta, (((0,), (0,)), ((), ())), preferred_element_type=f32
+    )
+
+
+def grad_products(hiddens, deltas):
+    width, cols = hiddens[0].shape[1], deltas[0].shape[1]
+    steps = 4
+    tile = width // steps
+    specs = [pl.BlockSpec((h.shape[0], tile), lambda j: (0, j)) for h in hiddens]
+    specs += [pl.BlockSpec(d.shape, lambda j: (0, 0)) for d in deltas]
     return pl.pallas_call(
-        turn_kernel,
-        grid=(width // tile,),
-        in_specs=[pl.BlockSpec((p.shape[0], tile), lambda j: (0, j)) for p in parts],
-        out_specs=pl.BlockSpec((tile, rows), lambda j: (j, 0)),
-        out_shape=jax.ShapeDtypeStruct((width, rows), bf16),
-        compiler_params=pltpu.CompilerParams(vmem_limit_bytes=VMEM_BYTES),
-        name="turned",
-    )(*parts)
+        grad_kernel,
+        grid=(steps,),
+        in_specs=specs,
+        out_specs=pl.BlockSpec((tile, cols), lambda j: (j, 0)),
+        out_shape=jax.ShapeDtypeStruct((width, cols), f32),
+        compiler_params=pltpu.CompilerParams(vmem_limit_bytes=GRAD_VMEM_BYTES),
+        cost_estimate=FREE,
+        name="grad_products",
+    )(*hiddens, *deltas)
 
 
 def paired_shards(tokens, gate_weight, up_weight, down_frozen, down_learn, steer, sample_lengths):
@@ -114,13 +132,18 @@
 
     other_tokens = swap("tensor", 1, tokens)
 
-    def given(w):
-        return lax.dynamic_slice_in_dim(w, (1 - core) * half, half, 1)
-
-    gate_give = given(gate_weight)
-    gate_sib = swap("fsdp", 1, gate_give)
-    up_give = given(after(up_weight, gate_give))
-    up_sib = swap("fsdp", 1, up_give)
+    def traded(w, sent):
+        depth = cols // SIB_PARTS
+        parts = []
+        for k in range(SIB_PARTS):
+            at = (k * depth, (1 - core) * half)
+            sent.append(lax.dynamic_slice(after(w, *sent[-1:]), at, (depth, half)))
+            parts.append(swap("fsdp", 1, sent[-1]))
+        return parts
+
+    sent = []
+    gate_sib = traded(gate_weight, sent)
+    up_sib = traded(up_weight, sent)
     weights = (gate_weight, up_weight, gate_sib, up_sib)
 
     lengths = jnp.where(forget_first, sample_lengths[0], sample_lengths[1])
@@ -137,12 +160,10 @@
         return (wanted[:, None] == position[None, :]).astype(bf16)
 
     mine = me_t % 2
-    mine_rows = dot(pick(mine), after(tokens, up_give))
-    other_tokens = after(other_tokens, up_give, mine_rows)
+    mine_rows = dot(pick(mine), after(tokens, sent[-1]))
+    other_tokens = after(other_tokens, mine_rows)
     x_a = (mine_rows + dot(pick(1 - mine), other_tokens)).astype(bf16)
-    hi_a, lo_a = x_a[quarter:], x_a[:quarter]
-    hi_b = swap("tensor", 3, hi_a)
-    lo_b = swap("tensor", 3, lo_a)
+    x_b = swap("tensor", 3, x_a)
     frozen_a = jnp.where(forget_first, 0.0, 1.0)
     frozen_b = 1.0 - frozen_a
     latest = []
@@ -156,40 +177,47 @@
         return x
 
     class Chunk:
-        def __init__(self, hi, lo):
-            self.hi, self.lo = hi, lo
-
-        def exchange_hi(self):
-            self.hi = go(self.hi)
-            self.hi_sib = swap("fsdp", 1, self.hi)
-
-        def exchange_lo(self):
-            self.lo = go(self.lo)
-            self.lo_sib = swap("fsdp", 1, self.lo)
-
-        def give(self):
-            hi = go(self.hi, self.hi_sib)
-            products = in_products(
-                core_arg, hi, lambda c: c, hi, lambda c: 2, weights, quarter, scale
+        def __init__(self, x):
+            self.x = x
+
+        def exchange(self):
+            self.x = did(go(self.x))
+            self.x_sib = swap("fsdp", 1, self.x)
+
+        def products(self, cost):
+            x, x_sib = go(self.x, self.x_sib)
+            self.give = did(
+                in_products(core_arg, x, x_sib, lambda c: 1 + c, lambda c: 3, weights, quarter, scale, cost)
             )
-            self.got = by_core(FIRST, did(products.astype(f16)))
-
-        def keep(self):
-            hi, lo = go(self.hi, self.hi_sib), (self.lo, self.lo_sib)
+
+        def send(self, apart):
+            give = go(self.give)
+            if apart:
+                gives = [give[0].astype(f16), give[1].astype(f16)]
+                did(gives[1])
+                self.got = [by_core(FIRST, g) for g in gives]
+            else:
+                got = by_core(FIRST, did(give.astype(f16)))
+                self.got = [got[0], got[1]]
+
+        def keep(self, cost):
+            x, x_sib = go(self.x, self.x_sib)
             self.kept = did(
-                in_products(core_arg, lo, lambda c: 0, hi, lambda c: 1 - c, weights, quarter, scale)
+                in_products(core_arg, x, x_sib, lambda c: 0, lambda c: 2 - c, weights, quarter, scale, cost)
             )
 
         def second(self):
-            got, kept = go(self.got, self.kept)
-            give = did((kept[:, quarter:] + got[:, quarter:].astype(f32)).astype(f16))
-            self.kept = kept[:, :quarter] + got[:, :quarter].astype(f32)
+            got0, got1, kept = go(*self.got, self.kept)
+            sums = [kept[0] + got0.astype(f32), kept[1] + got1.astype(f32)]
+            give = did(jnp.concatenate([s[quarter:] for s in sums], axis=0).astype(f16))
+            self.kept = [s[:quarter] for s in sums]
             self.got = by_core(SECOND, give)
 
         def hidden(self):
-            got, kept = go(self.got, self.kept)
-            summed = (kept + got.astype(f32)) * (1.0 / scale)
-            self.own = did((jax.nn.silu(summed[0]) * summed[1]).astype(bf16))
+            got, gate, up = go(self.got, *self.kept)
+            gate = (gate + got[:quarter].astype(f32)) * (1.0 / scale)
+            up = (up + got[quarter:].astype(f32)) * (1.0 / scale)
+            self.own = did((jax.nn.silu(gate) * up).astype(bf16))
             self.got = by_core(SECOND, self.own)
 
         def gather_half(self):
@@ -224,8 +252,12 @@
             own_rows_in = rows_of(low_half)
             give = did(mlp(other_rows).astype(bf16))
             self.got = swap("tensor", 1, give)
-            self.mlp = did(mlp(go(own_rows_in)))
             self.parts = [own_rows_in, other_rows]
+            self.rest = mlp
+
+        def down_rest(self):
+            self.mlp = did(self.rest(go(self.parts[0])))
+
 
         def pair(self):
             mlp, got = go(self.mlp, self.got)
@@ -235,8 +267,7 @@
         def delta(self, far):
             mlp, got, far = go(self.mlp, self.got, far)
             mlp = mlp + got.astype(f32) + far.astype(f32)
-            x = jnp.concatenate([self.lo, self.hi], axis=0)
-            base = jnp.where(low_half, x[:own_rows], x[own_rows:]).astype(f32)
+            base = jnp.where(low_half, self.x[:own_rows], self.x[own_rows:]).astype(f32)
             diff = jnp.where(forget_first, mlp, base + mlp - target[None, :])
             self.loss = jnp.sum(diff * diff)
             mine = did((diff * jnp.where(forget_first, 2.0, 1.0)).astype(bf16))
@@ -244,50 +275,52 @@
             self.delta_b = [mine, swap("tensor", 1, mine)]
 
         def turn_back(self):
-            back = go(self.back)
+            self.delta_b[1] = did(go(self.delta_b[1]))
+            back = did(go(self.back))
             self.delta_a = [back, swap("tensor", 1, back)]
 
     mean_square = jnp.mean(steer * steer)
     target_scale = 20.0 / jnp.sqrt(total * (mean_square + 1e-06))
     target = target_scale * lax.dynamic_slice_in_dim(steer, me_f * cols, cols)
 
-    a, b = Chunk(hi_a, lo_a), Chunk(hi_b, lo_b)
-    a.exchange_hi()
-    a.exchange_lo()
-    a.give()
-    b.exchange_hi()
-    a.keep()
+    a, b = Chunk(x_a), Chunk(x_b)
+    a.exchange()
+    a.products(FREE)
+    a.send(True)
+    a.keep(FREE)
+    b.exchange()
     a.second()
-    b.give()
-    b.exchange_lo()
+    b.products(FREE)
     a.hidden()
+    b.send(False)
     a.gather_half()
-    b.keep()
+    b.keep(FREE)
     a.gather_whole()
     b.second()
     a.down(frozen_a)
     b.hidden()
+    a.down_rest()
     b.gather_half()
     a.pair()
     b.gather_whole()
     b.down(frozen_b)
+    b.down_rest()
     b.delta(a.far)
     value = jnp.full((8, 128), b.loss, f32)
     value = did(value + go(swap("fsdp", 2, value)))
+    hiddens = go(*a.parts, *b.parts)
+    did(hiddens[0])
     b.turn_back()
-    value = did(value + go(swap("fsdp", 4, value)))
-    value = did(value + go(swap("fsdp", 1, value)))
-    value = did(value + go(swap("tensor", 1, value)))
-    other = swap("tensor", 3, value)
-    hidden = did(turned(list(go(*a.parts, *b.parts))))
-    delta = jnp.concatenate(b.delta_a + b.delta_b, axis=0)
-    grad_down = did(dot(go(hidden), delta))
-    other = go(other)
-    sum_steer = jnp.where(forget_first, other, value)[0, 0]
-    sum_keep = jnp.where(forget_first, value, other)[0, 0]
-    count_f = jnp.sum(sample_lengths[0]).astype(f32)
-    count_r = jnp.sum(sample_lengths[1]).astype(f32)
-    losses = jnp.stack([sum_steer / (count_f * total), sum_keep / (count_r * total)])
+    for bit in (4, 1):
+        value = did(value + go(swap("fsdp", bit, value)))
+    b.delta_a[1] = did(go(b.delta_a[1]))
+    others = [swap("tensor", bit, value) for bit in (1, 2, 3)]
+    grad_down = did(grad_products(hiddens, go(*b.delta_a, *b.delta_b)))
+    value, *others = go(value, *others)
+    same, other = (value + others[0])[0, :2], (others[1] + others[2])[0, :2]
+    steer_place = jnp.arange(2, dtype=jnp.int32) == 0
+    counts = jnp.sum(sample_lengths, axis=1).astype(f32) * total
+    losses = jnp.where(steer_place == forget_first, other, same) / counts
     return grad_down, losses
 
 

time: 193 us -> 180 us (0.933)
  matrix products: 25.2 us -> 13.1 us
  starting transfers between devices: 49.2 us -> 37.3 us
  Pallas kernels: 29.8 us -> 39.9 us
  local copies, waits for them, and re-layouts: 11.7 us -> 16.3 us
  waiting for transfers between devices: 55.3 us -> 52.4 us
  between operations: 4.54 us -> 1.9 us
  other arithmetic: 17 us -> 19 us
    ppermute x24, waiting for transfers between devices: 43.1 us -> 26.1 us  [swap(): lax.ppermute(x, axis, [(i, i ^ bit) for i in range(lax.axis_size(axis))])]
    ppermute x8 -> x9, waiting for transfers between devices: 12.2 us -> 26.3 us  [by_core(): lax.ppermute(x, 'fsdp', [(i, i ^ (odd if i % 2 else even)) for i in range...]
    ppermute x24, starting transfers between devices: 38.5 us -> 24.6 us  [swap(): lax.ppermute(x, axis, [(i, i ^ bit) for i in range(lax.axis_size(axis))])]
    dot_general x11 -> x10, matrix products: 25.2 us -> 13.1 us  [dot(): return jnp.dot(a, b, preferred_element_type=f32)]
    pallas_call x1, Pallas kernels: 2 us -> 10.7 us  [grad_products(): pl.pallas_call(grad_kernel, grid=(steps,), in_specs=specs, out_specs=pl.B...]
    dynamic_slice x2 -> x4, local copies, waits for them, and re-layouts: 6.44 us -> 8.94 us  [traded(): sent.append(lax.dynamic_slice(after(w, *sent[-1:]), at, (depth, half)))]
    ppermute x8 -> x9, starting transfers between devices: 10.7 us -> 12.7 us  [by_core(): lax.ppermute(x, 'fsdp', [(i, i ^ (odd if i % 2 else even)) for i in range...]
    unnamed x38 -> x40, local copies, waits for them, and re-layouts: 3.4 us -> 4.37 us
  transfers between devices with their start and end apart: 32 -> 33, of which waited for: 15 -> 16; matrix products, arithmetic and copies ran while one was open for 20% -> 24% of each run, Pallas kernels for 12% -> 22%
where the time goes in v2:
time: 180 us
  waiting for transfers between devices  52.4 us (29%)
  Pallas kernels  39.9 us (22%)
  starting transfers between devices  37.3 us (21%)
  other arithmetic  19 us (11%)
  local copies, waits for them, and re-layouts  16.3 us (9%)
  matrix products  13.1 us (7%)
  between operations  1.9 us (1%)
    pallas_call x4, Pallas kernels, in_products(): pl.pallas_call(lambda *refs: in_kernel(*refs, scale=scale), grid_spec=plt...  29.1 us
    ppermute x9, waiting for transfers between devices, by_core(): lax.ppermute(x, 'fsdp', [(i, i ^ (odd if i % 2 else even)) for i in range...  26.3 us
    ppermute x24, waiting for transfers between devices, swap(): lax.ppermute(x, axis, [(i, i ^ bit) for i in range(lax.axis_size(axis))])  26.1 us
    ppermute x24, starting transfers between devices, swap(): lax.ppermute(x, axis, [(i, i ^ bit) for i in range(lax.axis_size(axis))])  24.6 us
    dot_general x10, matrix products, dot(): return jnp.dot(a, b, preferred_element_type=f32)  13.1 us
    ppermute x9, starting transfers between devices, by_core(): lax.ppermute(x, 'fsdp', [(i, i ^ (odd if i % 2 else even)) for i in range...  12.7 us
    pallas_call x1, Pallas kernels, grad_products(): pl.pallas_call(grad_kernel, grid=(steps,), in_specs=specs, out_specs=pl.B...  10.7 us
    dynamic_slice x4, local copies, waits for them, and re-layouts, traded(): sent.append(lax.dynamic_slice(after(w, *sent[-1:]), at, (depth, half)))  8.94 us
  transfers between devices with their start and end apart: 33, of which 16 were waited for; matrix products, arithmetic and copies ran while one was open for 24% of the time, Pallas kernels for 22%

profile of v2, /device:TPU:0, one launch (start us, length us, event | category | flops | bytes accessed | tf_op | source)
XLA Modules:
  0.0 179.7 jit_solution(2557870103857807528)
XLA Ops:
  0.6 3.1 %collective-permute-start = (bf16[256,1024]{1,0:T(8,128)(2,1)}, bf16[256,1024]{1,0:T(8,128)(2,1)S(1)}, u32[]{:S(2)}, u32[]{:S(2)}) collective-permute-start(bf16[256,1024]{1,0:T(8,128)(2,1)} %param.7), channel_id=1, source_target_pairs={{0,1},{1,0},{2,3},{3,2},{4,5},{5,4},{6,7},{7,6},{8,9},{9,8},{10,11... | collective-permute-start | bytes 1572872 | tf_op jit(solution)/shard_map/ppermute | solution.py:36
  3.7 3.0 %constant_dynamic-slice_fusion.3 = bf16[512,1792]{1,0:T(8,128)(2,1)} fusion(bf16[1024,3584]{1,0:T(8,128)(2,1)} %refs_5_.7, s32[]{:T(128)S(6)} %select_n.296), kind=kLoop, calls=%fused_computation.127 | loop fusion | bytes 3670020 | tf_op jit(solution)/shard_map/dynamic_slice | solution.py:140
  6.7 3.2 %constant_dynamic-slice_fusion.1 = bf16[512,1792]{1,0:T(8,128)(2,1)} fusion(bf16[1024,3584]{1,0:T(8,128)(2,1)} %refs_5_.7, s32[]{:T(128)S(6)} %select_n.296), kind=kLoop, calls=%fused_computation.121 | loop fusion | bytes 3670020 | tf_op jit(solution)/shard_map/dynamic_slice | solution.py:140
  14.2 1.7 collective-permute-done
  16.3 3.5 %collective-permute-done.1.refs_3_.refs_4_ = bf16[320,1024]{1,0:T(8,128)(2,1)S(1)} collective-permute-done((bf16[320,1024]{1,0:T(8,128)(2,1)S(1)}, bf16[320,1024]{1,0:T(8,128)(2,1)S(1)}, u32[]{:S(2)}, u32[]{:S(2)}) %collective-permute-start.1) | collective-permute-done | bytes 655392 | tf_op jit(solution)/shard_map/ppermute | solution.py:36
  19.9 2.5 %collective-permute-start.8 = (bf16[320,1024]{1,0:T(8,128)(2,1)S(1)}, bf16[320,1024]{1,0:T(8,128)(2,1)S(1)}, u32[]{:S(2)}, u32[]{:S(2)}) collective-permute-start(bf16[320,1024]{1,0:T(8,128)(2,1)S(1)} %fusion.refs_1_.refs_2_), channel_id=1, source_target_pairs={{0,3},{1,2},{2,1},{3,0},{4,7},{5,6},{6,5},{7,4},{8,11},{9,10},{10,... | collective-permute-start | bytes 1966088 | tf_op jit(solution)/shard_map/ppermute | solution.py:36
  22.4 7.3 %in_products.4 = f32[2,160,1792]{2,1,0:T(8,128)} custom-call(s32[1]{0:T(128)} %bitcast.refs_0_, bf16[320,1024]{1,0:T(8,128)(2,1)S(1)} %fusion.refs_1_.refs_2_, bf16[320,1024]{1,0:T(8,128)(2,1)S(1)} %fusion.refs_1_.refs_2_, bf16[320,1024]{1,0:T(8,128)(2,1)S(1)} %collective-permute-done.1.refs_3_.refs_4_, ...), custom_call_target="tpu_custom_call" | custom-call | tf_op jit(solution)/shard_map/in_products/pallas_call | solution.py:72
  29.7 1.8 convert.20
  33.7 7.3 %in_products.5 = f32[2,160,1792]{2,1,0:T(8,128)} custom-call(s32[1]{0:T(128)} %bitcast.refs_0_, bf16[320,1024]{1,0:T(8,128)(2,1)S(1)} %fusion.refs_1_.refs_2_, bf16[320,1024]{1,0:T(8,128)(2,1)S(1)} %fusion.refs_1_.refs_2_, bf16[320,1024]{1,0:T(8,128)(2,1)S(1)} %collective-permute-done.1.refs_3_.refs_4_, ...), custom_call_target="tpu_custom_call" | custom-call | tf_op jit(solution)/shard_map/in_products/pallas_call | solution.py:72
  41.4 6.1 %collective-permute-done.7 = f16[160,1792]{1,0:T(8,128)(2,1)S(1)} collective-permute-done((f16[160,1792]{1,0:T(8,128)(2,1)S(1)}, f16[160,1792]{1,0:T(8,128)(2,1)S(1)}, u32[]{:S(2)}, u32[]{:S(2)}) %collective-permute-start.7) | collective-permute-done | bytes 573472 | tf_op jit(solution)/shard_map/ppermute | solution.py:42
  47.5 1.9 %bitcast_add_fusion.3 = (f32[160,1792]{1,0:T(8,128)S(1)}, f32[160,1792]{1,0:T(8,128)S(1)}) fusion(f16[160,1792]{1,0:T(8,128)(2,1)S(1)} %collective-permute-done.6, f32[2,160,1792]{2,1,0:T(8,128)} %in_products.5, f16[160,1792]{1,0:T(8,128)(2,1)S(1)} %collective-permute-done.7), kind=kLoop, calls=%fused_computation.19 | loop fusion | flops 1146880 | bytes 5734400 | tf_op jit(solution)/shard_map/add | solution.py:211
  49.7 1.6 collective-permute-start.9
  51.3 7.3 %in_products.6 = f32[2,160,1792]{2,1,0:T(8,128)} custom-call(s32[1]{0:T(128)} %bitcast.refs_0_, bf16[320,1024]{1,0:T(8,128)(2,1)S(1)} %collective-permute-done.8.refs_1_.refs_2_, bf16[320,1024]{1,0:T(8,128)(2,1)S(1)} %collective-permute-done.8.refs_1_.refs_2_, bf16[320,1024]{1,0:T(8,128)(2,1)S(1)} %collective-permute-done.10.refs_3_.refs_4_, ...), custom_call_target="tpu_custom_call" | custom-call | tf_op jit(solution)/shard_map/in_products/pallas_call | solution.py:72
  59.8 1.6 collective-permute-start.11
  61.3 2.8 %convert_element_type.83 = f16[2,160,1792]{2,1,0:T(8,128)(2,1)} convert(f32[2,160,1792]{2,1,0:T(8,128)} %in_products.6) | non-fusion elementwise | flops 573440 | bytes 3440640 | tf_op jit(solution)/shard_map/convert_element_type | solution.py:200
  65.6 2.4 %collective-permute-done.11 = bf16[80,1792]{1,0:T(8,128)(2,1)S(1)} collective-permute-done((bf16[80,1792]{1,0:T(8,128)(2,1)S(1)}, bf16[80,1792]{1,0:T(8,128)(2,1)S(1)}, u32[]{:S(2)}, u32[]{:S(2)}) %collective-permute-start.11) | collective-permute-done | bytes 286752 | tf_op jit(solution)/shard_map/ppermute | solution.py:42
  69.5 2.6 %collective-permute-start.12 = (bf16[160,1792]{1,0:T(8,128)(2,1)}, bf16[160,1792]{1,0:T(8,128)(2,1)}, u32[]{:S(2)}, u32[]{:S(2)}) collective-permute-start(bf16[160,1792]{1,0:T(8,128)(2,1)} %constant_dynamic-update-slice_fusion), channel_id=1, source_target_pairs={{0,8},{4,20},{8,0},{12,28},{16,24},{20,4},{24,16},{28,12},{1,9},{5... | collective-permute-start | bytes 1720328 | tf_op jit(solution)/shard_map/ppermute | solution.py:42
  72.1 7.3 %in_products.7 = f32[2,160,1792]{2,1,0:T(8,128)} custom-call(s32[1]{0:T(128)} %bitcast.refs_0_, bf16[320,1024]{1,0:T(8,128)(2,1)S(1)} %collective-permute-done.8.refs_1_.refs_2_, bf16[320,1024]{1,0:T(8,128)(2,1)S(1)} %collective-permute-done.8.refs_1_.refs_2_, bf16[320,1024]{1,0:T(8,128)(2,1)S(1)} %collective-permute-done.10.refs_3_.refs_4_, ...), custom_call_target="tpu_custom_call" | custom-call | tf_op jit(solution)/shard_map/in_products/pallas_call | solution.py:72
  79.3 7.1 %collective-permute-done.12 = bf16[160,1792]{1,0:T(8,128)(2,1)} collective-permute-done((bf16[160,1792]{1,0:T(8,128)(2,1)}, bf16[160,1792]{1,0:T(8,128)(2,1)}, u32[]{:S(2)}, u32[]{:S(2)}) %collective-permute-start.12) | collective-permute-done | bytes 573472 | tf_op jit(solution)/shard_map/ppermute | solution.py:42
  89.0 1.7 broadcast_select_fusion.23
  94.9 2.1 %fusion.6 = bf16[160,1024]{1,0:T(8,128)(2,1)} fusion(f32[160,1024]{1,0:T(8,128)S(1)} %fusion.28, bf16[3584,1024]{1,0:T(8,128)(2,1)S(1)} %bitcast.44, f32[]{:T(128)S(6)} %select_n.317, bf16[160,1792]{1,0:T(8,128)(2,1)S(1)} %get-tuple-element.148, bf16[160,1792]{1,0:T(8,128)(2,1)S(1)} %get-tuple-element.146), kind=kOutput, calls=%fused_computation.11 | convolution fusion | flops 1177190400 | bytes 9469956 | tf_op jit(solution)/shard_map/dot_general | solution.py:32
  97.1 4.6 %collective-permute-start.19 = (bf16[160,1024]{1,0:T(8,128)(2,1)}, bf16[160,1024]{1,0:T(8,128)(2,1)S(1)}, u32[]{:S(2)}, u32[]{:S(2)}) collective-permute-start(bf16[160,1024]{1,0:T(8,128)(2,1)} %fusion.6), channel_id=1, source_target_pairs={{0,1},{1,0},{2,3},{3,2},{4,5},{5,4},{6,7},{7,6},{8,9},{9,8},{10,11... | collective-permute-start | bytes 983048 | tf_op jit(solution)/shard_map/ppermute | solution.py:36
  106.2 2.5 %collective-permute-done.17 = bf16[80,1792]{1,0:T(8,128)(2,1)S(1)} collective-permute-done((bf16[80,1792]{1,0:T(8,128)(2,1)S(1)}, bf16[80,1792]{1,0:T(8,128)(2,1)S(1)}, u32[]{:S(2)}, u32[]{:S(2)}) %collective-permute-start.17) | collective-permute-done | bytes 286752 | tf_op jit(solution)/shard_map/ppermute | solution.py:42
  111.9 6.8 %collective-permute-done.18 = bf16[160,1792]{1,0:T(8,128)(2,1)} collective-permute-done((bf16[160,1792]{1,0:T(8,128)(2,1)S(1)}, bf16[160,1792]{1,0:T(8,128)(2,1)}, u32[]{:S(2)}, u32[]{:S(2)}) %collective-permute-start.18) | collective-permute-done | bytes 573472 | tf_op jit(solution)/shard_map/ppermute | solution.py:42
  119.8 2.6 %collective-permute-start.23 = (bf16[160,1024]{1,0:T(8,128)(2,1)S(1)}, bf16[160,1024]{1,0:T(8,128)(2,1)S(1)}, u32[]{:S(2)}, u32[]{:S(2)}) collective-permute-start(bf16[160,1024]{1,0:T(8,128)(2,1)S(1)} %add_convert_fusion), channel_id=1, source_target_pairs={{0,3},{1,2},{2,1},{3,0},{4,7},{5,6},{6,5},{7,4},{8,11},{9,10},{10,... | collective-permute-start | bytes 983048 | tf_op jit(solution)/shard_map/ppermute | solution.py:36
  128.8 1.7 fusion.34
  132.2 6.7 %collective-permute-done.22 = bf16[160,1024]{1,0:T(8,128)(2,1)S(1)} collective-permute-done((bf16[160,1024]{1,0:T(8,128)(2,1)S(1)}, bf16[160,1024]{1,0:T(8,128)(2,1)S(1)}, u32[]{:S(2)}, u32[]{:S(2)}) %collective-permute-start.22) | collective-permute-done | bytes 327712 | tf_op jit(solution)/shard_map/ppermute | solution.py:36
  140.0 1.9 %collective-permute-start.25 = (bf16[160,1024]{1,0:T(8,128)(2,1)S(1)}, bf16[160,1024]{1,0:T(8,128)(2,1)S(1)}, u32[]{:S(2)}, u32[]{:S(2)}) collective-permute-start(bf16[160,1024]{1,0:T(8,128)(2,1)S(1)} %get-tuple-element.128.refs_6_), channel_id=1, source_target_pairs={{0,3},{1,2},{2,1},{3,0},{4,7},{5,6},{6,5},{7,4},{8,11},{9,10},{10,... | collective-permute-start | bytes 983048 | tf_op jit(solution)/shard_map/ppermute | solution.py:36
  148.7 8.3 %collective-permute-done.25.refs_4_ = bf16[160,1024]{1,0:T(8,128)(2,1)S(1)} collective-permute-done((bf16[160,1024]{1,0:T(8,128)(2,1)S(1)}, bf16[160,1024]{1,0:T(8,128)(2,1)S(1)}, u32[]{:S(2)}, u32[]{:S(2)}) %collective-permute-start.25) | collective-permute-done | bytes 327712 | tf_op jit(solution)/shard_map/ppermute | solution.py:36
  158.8 2.5 %collective-permute-done.28 = f32[8,128]{1,0:T(8,128)S(1)} collective-permute-done((f32[8,128]{1,0:T(8,128)S(1)}, f32[8,128]{1,0:T(8,128)S(1)}, u32[]{:S(2)}, u32[]{:S(2)}) %collective-permute-start.28) | collective-permute-done | bytes 4128 | tf_op jit(solution)/shard_map/ppermute | solution.py:36
  164.5 1.9 %collective-permute-start.31 = (f32[8,128]{1,0:T(8,128)S(1)}, f32[8,128]{1,0:T(8,128)S(1)}, u32[]{:S(2)}, u32[]{:S(2)}) collective-permute-start(f32[8,128]{1,0:T(8,128)S(1)} %add.210), channel_id=1, source_target_pairs={{0,2},{1,3},{2,0},{3,1},{4,6},{5,7},{6,4},{7,5},{8,10},{9,11},{10,... | collective-permute-start | bytes 12296 | tf_op jit(solution)/shard_map/ppermute | solution.py:36
  168.4 10.7 %grad_products.1 = f32[3584,1024]{1,0:T(8,128)} custom-call(bf16[160,3584]{1,0:T(8,128)(2,1)} %copy-done.1, bf16[160,3584]{1,0:T(8,128)(2,1)} %pad_maximum_fusion.1.refs_1_, bf16[160,3584]{1,0:T(8,128)(2,1)} %copy-done.2, bf16[160,3584]{1,0:T(8,128)(2,1)} %pad_maximum_fusion.3.refs_3_, bf16[160,1024]{1,0:T(8,128)(2,1)} %copy-done.7, ...), custom_call_target="tpu_custom_call" | custom-call | tf_op jit(solution)/shard_map/grad_products/pallas_call | solution.py:103
  (147 shorter events, 49.7 us)
Async XLA Ops:
  0.6 15.2 %collective-permute-start = (bf16[256,1024]{1,0:T(8,128)(2,1)}, bf16[256,1024]{1,0:T(8,128)(2,1)S(1)}, u32[]{:S(2)}, u32[]{:S(2)}) collective-permute-start(bf16[256,1024]{1,0:T(8,128)(2,1)} %param.7), channel_id=1, source_target_pairs={{0,1},{1,0},{2,3},{3,2},{4,5},{5,4},{6,7},{7,6},{8,9},{9,8},{10,11... | collective-permute-start | bytes 1572872 | tf_op jit(solution)/shard_map/ppermute | solution.py:36
  6.7 15.6 %collective-permute-start.2 = (bf16[512,1792]{1,0:T(8,128)(2,1)}, bf16[512,1792]{1,0:T(8,128)(2,1)S(1)}, u32[]{:S(2)}, u32[]{:S(2)}) collective-permute-start(bf16[512,1792]{1,0:T(8,128)(2,1)} %constant_dynamic-slice_fusion.3), channel_id=1, source_target_pairs={{0,4},{4,0},{8,12},{12,8},{16,20},{20,16},{24,28},{28,24},{1,5},{5... | collective-permute-start | bytes 5505032 | tf_op jit(solution)/shard_map/ppermute | solution.py:36
  9.9 12.5 %collective-permute-start.3 = (bf16[512,1792]{1,0:T(8,128)(2,1)}, bf16[512,1792]{1,0:T(8,128)(2,1)}, u32[]{:S(2)}, u32[]{:S(2)}) collective-permute-start(bf16[512,1792]{1,0:T(8,128)(2,1)} %constant_dynamic-slice_fusion.1), channel_id=1, source_target_pairs={{0,4},{4,0},{8,12},{12,8},{16,20},{20,16},{24,28},{28,24},{1,5},{5... | collective-permute-start | bytes 5505032 | tf_op jit(solution)/shard_map/ppermute | solution.py:36
  11.5 10.8 %collective-permute-start.4 = (bf16[512,1792]{1,0:T(8,128)(2,1)}, bf16[512,1792]{1,0:T(8,128)(2,1)}, u32[]{:S(2)}, u32[]{:S(2)}) collective-permute-start(bf16[512,1792]{1,0:T(8,128)(2,1)} %constant_dynamic-slice_fusion.2), channel_id=1, source_target_pairs={{0,4},{4,0},{8,12},{12,8},{16,20},{20,16},{24,28},{28,24},{1,5},{5... | collective-permute-start | bytes 5505032 | tf_op jit(solution)/shard_map/ppermute | solution.py:36
  13.2 9.2 %collective-permute-start.5 = (bf16[512,1792]{1,0:T(8,128)(2,1)}, bf16[512,1792]{1,0:T(8,128)(2,1)}, u32[]{:S(2)}, u32[]{:S(2)}) collective-permute-start(bf16[512,1792]{1,0:T(8,128)(2,1)} %constant_dynamic-slice_fusion), channel_id=1, source_target_pairs={{0,4},{4,0},{8,12},{12,8},{16,20},{20,16},{24,28},{28,24},{1,5},{5... | collective-permute-start | bytes 5505032 | tf_op jit(solution)/shard_map/ppermute | solution.py:36
  16.2 3.6 %collective-permute-start.1 = (bf16[320,1024]{1,0:T(8,128)(2,1)S(1)}, bf16[320,1024]{1,0:T(8,128)(2,1)S(1)}, u32[]{:S(2)}, u32[]{:S(2)}) collective-permute-start(bf16[320,1024]{1,0:T(8,128)(2,1)S(1)} %fusion.refs_1_.refs_2_), channel_id=1, source_target_pairs={{0,4},{4,0},{8,12},{12,8},{16,20},{20,16},{24,28},{28,24},{1,5},{5... | collective-permute-start | bytes 1966088 | tf_op jit(solution)/shard_map/ppermute | solution.py:36
  19.9 21.1 %collective-permute-start.8 = (bf16[320,1024]{1,0:T(8,128)(2,1)S(1)}, bf16[320,1024]{1,0:T(8,128)(2,1)S(1)}, u32[]{:S(2)}, u32[]{:S(2)}) collective-permute-start(bf16[320,1024]{1,0:T(8,128)(2,1)S(1)} %fusion.refs_1_.refs_2_), channel_id=1, source_target_pairs={{0,3},{1,2},{2,1},{3,0},{4,7},{5,6},{6,5},{7,4},{8,11},{9,10},{10,... | collective-permute-start | bytes 1966088 | tf_op jit(solution)/shard_map/ppermute | solution.py:36
  31.6 9.8 %collective-permute-start.6 = (f16[160,1792]{1,0:T(8,128)(2,1)S(1)}, f16[160,1792]{1,0:T(8,128)(2,1)S(1)}, u32[]{:S(2)}, u32[]{:S(2)}) collective-permute-start(f16[160,1792]{1,0:T(8,128)(2,1)S(1)} %get-tuple-element.173), channel_id=1, source_target_pairs={{0,8},{4,20},{8,0},{12,28},{16,24},{20,4},{24,16},{28,12},{1,9},{5... | collective-permute-start | bytes 1720328 | tf_op jit(solution)/shard_map/ppermute | solution.py:42
  33.2 14.4 %collective-permute-start.7 = (f16[160,1792]{1,0:T(8,128)(2,1)S(1)}, f16[160,1792]{1,0:T(8,128)(2,1)S(1)}, u32[]{:S(2)}, u32[]{:S(2)}) collective-permute-start(f16[160,1792]{1,0:T(8,128)(2,1)S(1)} %get-tuple-element.172), channel_id=1, source_target_pairs={{0,8},{4,20},{8,0},{12,28},{16,24},{20,4},{24,16},{28,12},{1,9},{5... | collective-permute-start | bytes 1720328 | tf_op jit(solution)/shard_map/ppermute | solution.py:42
  41.0 10.3 %collective-permute-start.10 = (bf16[320,1024]{1,0:T(8,128)(2,1)S(1)}, bf16[320,1024]{1,0:T(8,128)(2,1)S(1)}, u32[]{:S(2)}, u32[]{:S(2)}) collective-permute-start(bf16[320,1024]{1,0:T(8,128)(2,1)S(1)} %collective-permute-done.8.refs_1_.refs_2_), channel_id=1, source_target_pairs={{0,4},{4,0},{8,12},{12,8},{16,20},{20,16},{24,28},{28,24},{1,5},{5... | collective-permute-start | bytes 1966088 | tf_op jit(solution)/shard_map/ppermute | solution.py:36
  49.7 9.8 %collective-permute-start.9 = (f16[160,1792]{1,0:T(8,128)(2,1)S(1)}, f16[160,1792]{1,0:T(8,128)(2,1)S(1)}, u32[]{:S(2)}, u32[]{:S(2)}) collective-permute-start(f16[160,1792]{1,0:T(8,128)(2,1)S(1)} %pad_maximum_fusion.4), channel_id=1, source_target_pairs={{0,16},{4,12},{8,24},{12,4},{16,0},{20,28},{24,8},{28,20},{1,17},{... | collective-permute-start | bytes 1720328 | tf_op jit(solution)/shard_map/ppermute | solution.py:42
  59.8 8.2 %collective-permute-start.11 = (bf16[80,1792]{1,0:T(8,128)(2,1)S(1)}, bf16[80,1792]{1,0:T(8,128)(2,1)S(1)}, u32[]{:S(2)}, u32[]{:S(2)}) collective-permute-start(bf16[80,1792]{1,0:T(8,128)(2,1)S(1)} %multiply_convert_fusion.2), channel_id=1, source_target_pairs={{0,16},{4,12},{8,24},{12,4},{16,0},{20,28},{24,8},{28,20},{1,17},{... | collective-permute-start | bytes 860168 | tf_op jit(solution)/shard_map/ppermute | solution.py:42
  64.1 22.3 %collective-permute-start.15 = (f16[2,160,1792]{2,1,0:T(8,128)(2,1)}, f16[2,160,1792]{2,1,0:T(8,128)(2,1)}, u32[]{:S(2)}, u32[]{:S(2)}) collective-permute-start(f16[2,160,1792]{2,1,0:T(8,128)(2,1)} %convert_element_type.83), channel_id=1, source_target_pairs={{0,8},{4,20},{8,0},{12,28},{16,24},{20,4},{24,16},{28,12},{1,9},{5... | collective-permute-start | bytes 3440648 | tf_op jit(solution)/shard_map/ppermute | solution.py:42
  69.5 17.0 %collective-permute-start.12 = (bf16[160,1792]{1,0:T(8,128)(2,1)}, bf16[160,1792]{1,0:T(8,128)(2,1)}, u32[]{:S(2)}, u32[]{:S(2)}) collective-permute-start(bf16[160,1792]{1,0:T(8,128)(2,1)} %constant_dynamic-update-slice_fusion), channel_id=1, source_target_pairs={{0,8},{4,20},{8,0},{12,28},{16,24},{20,4},{24,16},{28,12},{1,9},{5... | collective-permute-start | bytes 1720328 | tf_op jit(solution)/shard_map/ppermute | solution.py:42
  72.1 17.0 %collective-permute-start.13 = (bf16[160,1792]{1,0:T(8,128)(2,1)}, bf16[160,1792]{1,0:T(8,128)(2,1)S(1)}, u32[]{:S(2)}, u32[]{:S(2)}) collective-permute-start(bf16[160,1792]{1,0:T(8,128)(2,1)} %constant_dynamic-update-slice_fusion), channel_id=1, source_target_pairs={{0,4},{4,0},{8,12},{12,8},{16,20},{20,16},{24,28},{28,24},{1,5},{5... | collective-permute-start | bytes 1720328 | tf_op jit(solution)/shard_map/ppermute | solution.py:36
  86.4 2.6 %collective-permute-start.14 = (bf16[160,1792]{1,0:T(8,128)(2,1)}, bf16[160,1792]{1,0:T(8,128)(2,1)S(1)}, u32[]{:S(2)}, u32[]{:S(2)}) collective-permute-start(bf16[160,1792]{1,0:T(8,128)(2,1)} %collective-permute-done.12), channel_id=1, source_target_pairs={{0,4},{4,0},{8,12},{12,8},{16,20},{20,16},{24,28},{28,24},{1,5},{5... | collective-permute-start | bytes 1720328 | tf_op jit(solution)/shard_map/ppermute | solution.py:36
  88.4 13.4 %collective-permute-start.16 = (f16[160,1792]{1,0:T(8,128)(2,1)S(1)}, f16[160,1792]{1,0:T(8,128)(2,1)S(1)}, u32[]{:S(2)}, u32[]{:S(2)}) collective-permute-start(f16[160,1792]{1,0:T(8,128)(2,1)S(1)} %pad_maximum_fusion.5), channel_id=1, source_target_pairs={{0,16},{4,12},{8,24},{12,4},{16,0},{20,28},{24,8},{28,20},{1,17},{... | collective-permute-start | bytes 1720328 | tf_op jit(solution)/shard_map/ppermute | solution.py:42
  97.1 14.7 %collective-permute-start.19 = (bf16[160,1024]{1,0:T(8,128)(2,1)}, bf16[160,1024]{1,0:T(8,128)(2,1)S(1)}, u32[]{:S(2)}, u32[]{:S(2)}) collective-permute-start(bf16[160,1024]{1,0:T(8,128)(2,1)} %fusion.6), channel_id=1, source_target_pairs={{0,1},{1,0},{2,3},{3,2},{4,5},{5,4},{6,7},{7,6},{8,9},{9,8},{10,11... | collective-permute-start | bytes 983048 | tf_op jit(solution)/shard_map/ppermute | solution.py:36
  102.1 6.7 %collective-permute-start.17 = (bf16[80,1792]{1,0:T(8,128)(2,1)S(1)}, bf16[80,1792]{1,0:T(8,128)(2,1)S(1)}, u32[]{:S(2)}, u32[]{:S(2)}) collective-permute-start(bf16[80,1792]{1,0:T(8,128)(2,1)S(1)} %multiply_convert_fusion.1), channel_id=1, source_target_pairs={{0,16},{4,12},{8,24},{12,4},{16,0},{20,28},{24,8},{28,20},{1,17},{... | collective-permute-start | bytes 860168 | tf_op jit(solution)/shard_map/ppermute | solution.py:42
  108.8 9.9 %collective-permute-start.18 = (bf16[160,1792]{1,0:T(8,128)(2,1)S(1)}, bf16[160,1792]{1,0:T(8,128)(2,1)}, u32[]{:S(2)}, u32[]{:S(2)}) collective-permute-start(bf16[160,1792]{1,0:T(8,128)(2,1)S(1)} %constant_dynamic-update-slice_fusion.2), channel_id=1, source_target_pairs={{0,8},{4,20},{8,0},{12,28},{16,24},{20,4},{24,16},{28,12},{1,9},{5... | collective-permute-start | bytes 1720328 | tf_op jit(solution)/shard_map/ppermute | solution.py:42
  111.7 10.8 %collective-permute-start.20 = (bf16[160,1792]{1,0:T(8,128)(2,1)S(1)}, bf16[160,1792]{1,0:T(8,128)(2,1)S(1)}, u32[]{:S(2)}, u32[]{:S(2)}) collective-permute-start(bf16[160,1792]{1,0:T(8,128)(2,1)S(1)} %constant_dynamic-update-slice_fusion.2), channel_id=1, source_target_pairs={{0,4},{4,0},{8,12},{12,8},{16,20},{20,16},{24,28},{28,24},{1,5},{5... | collective-permute-start | bytes 1720328 | tf_op jit(solution)/shard_map/ppermute | solution.py:36
  118.7 3.8 %collective-permute-start.21 = (bf16[160,1792]{1,0:T(8,128)(2,1)}, bf16[160,1792]{1,0:T(8,128)(2,1)S(1)}, u32[]{:S(2)}, u32[]{:S(2)}) collective-permute-start(bf16[160,1792]{1,0:T(8,128)(2,1)} %collective-permute-done.18), channel_id=1, source_target_pairs={{0,4},{4,0},{8,12},{12,8},{16,20},{20,16},{24,28},{28,24},{1,5},{5... | collective-permute-start | bytes 1720328 | tf_op jit(solution)/shard_map/ppermute | solution.py:36
  119.8 12.4 %collective-permute-start.23 = (bf16[160,1024]{1,0:T(8,128)(2,1)S(1)}, bf16[160,1024]{1,0:T(8,128)(2,1)S(1)}, u32[]{:S(2)}, u32[]{:S(2)}) collective-permute-start(bf16[160,1024]{1,0:T(8,128)(2,1)S(1)} %add_convert_fusion), channel_id=1, source_target_pairs={{0,3},{1,2},{2,1},{3,0},{4,7},{5,6},{6,5},{7,4},{8,11},{9,10},{10,... | collective-permute-start | bytes 983048 | tf_op jit(solution)/shard_map/ppermute | solution.py:36
  128.5 10.4 %collective-permute-start.22 = (bf16[160,1024]{1,0:T(8,128)(2,1)S(1)}, bf16[160,1024]{1,0:T(8,128)(2,1)S(1)}, u32[]{:S(2)}, u32[]{:S(2)}) collective-permute-start(bf16[160,1024]{1,0:T(8,128)(2,1)S(1)} %fusion.5), channel_id=1, source_target_pairs={{0,1},{1,0},{2,3},{3,2},{4,5},{5,4},{6,7},{7,6},{8,9},{9,8},{10,11... | collective-permute-start | bytes 983048 | tf_op jit(solution)/shard_map/ppermute | solution.py:36
  139.2 9.5 %collective-permute-start.26 = (bf16[160,1024]{1,0:T(8,128)(2,1)S(1)}, bf16[160,1024]{1,0:T(8,128)(2,1)S(1)}, u32[]{:S(2)}, u32[]{:S(2)}) collective-permute-start(bf16[160,1024]{1,0:T(8,128)(2,1)S(1)} %get-tuple-element.128.refs_6_), channel_id=1, source_target_pairs={{0,1},{1,0},{2,3},{3,2},{4,5},{5,4},{6,7},{7,6},{8,9},{9,8},{10,11... | collective-permute-start | bytes 983048 | tf_op jit(solution)/shard_map/ppermute | solution.py:36
  140.0 16.9 %collective-permute-start.25 = (bf16[160,1024]{1,0:T(8,128)(2,1)S(1)}, bf16[160,1024]{1,0:T(8,128)(2,1)S(1)}, u32[]{:S(2)}, u32[]{:S(2)}) collective-permute-start(bf16[160,1024]{1,0:T(8,128)(2,1)S(1)} %get-tuple-element.128.refs_6_), channel_id=1, source_target_pairs={{0,3},{1,2},{2,1},{3,0},{4,7},{5,6},{6,5},{7,4},{8,11},{9,10},{10,... | collective-permute-start | bytes 983048 | tf_op jit(solution)/shard_map/ppermute | solution.py:36
  143.4 3.7 %collective-permute-start.24 = (f32[8,128]{1,0:T(8,128)S(1)}, f32[8,128]{1,0:T(8,128)S(1)}, u32[]{:S(2)}, u32[]{:S(2)}) collective-permute-start(f32[8,128]{1,0:T(8,128)S(1)} %broadcast_in_dim.58), channel_id=1, source_target_pairs={{0,8},{4,12},{8,0},{12,4},{16,24},{20,28},{24,16},{28,20},{1,9},{5... | collective-permute-start | bytes 12296 | tf_op jit(solution)/shard_map/ppermute | solution.py:36
  156.9 10.7 %collective-permute-start.27 = (bf16[160,1024]{1,0:T(8,128)(2,1)S(1)}, bf16[160,1024]{1,0:T(8,128)(2,1)S(1)}, u32[]{:S(2)}, u32[]{:S(2)}) collective-permute-start(bf16[160,1024]{1,0:T(8,128)(2,1)S(1)} %collective-permute-done.25.refs_4_), channel_id=1, source_target_pairs={{0,1},{1,0},{2,3},{3,2},{4,5},{5,4},{6,7},{7,6},{8,9},{9,8},{10,11... | collective-permute-start | bytes 983048 | tf_op jit(solution)/shard_map/ppermute | solution.py:36
  157.7 3.6 %collective-permute-start.28 = (f32[8,128]{1,0:T(8,128)S(1)}, f32[8,128]{1,0:T(8,128)S(1)}, u32[]{:S(2)}, u32[]{:S(2)}) collective-permute-start(f32[8,128]{1,0:T(8,128)S(1)} %broadcast_add_fusion), channel_id=1, source_target_pairs={{0,16},{4,20},{8,24},{12,28},{16,0},{20,4},{24,8},{28,12},{1,17},{... | collective-permute-start | bytes 12296 | tf_op jit(solution)/shard_map/ppermute | solution.py:36
  163.2 16.0 %collective-permute-start.30 = (f32[8,128]{1,0:T(8,128)S(1)}, f32[8,128]{1,0:T(8,128)S(1)}, u32[]{:S(2)}, u32[]{:S(2)}) collective-permute-start(f32[8,128]{1,0:T(8,128)S(1)} %add.210), channel_id=1, source_target_pairs={{0,1},{1,0},{2,3},{3,2},{4,5},{5,4},{6,7},{7,6},{8,9},{9,8},{10,11... | collective-permute-start | bytes 12296 | tf_op jit(solution)/shard_map/ppermute | solution.py:36
  164.5 14.7 %collective-permute-start.31 = (f32[8,128]{1,0:T(8,128)S(1)}, f32[8,128]{1,0:T(8,128)S(1)}, u32[]{:S(2)}, u32[]{:S(2)}) collective-permute-start(f32[8,128]{1,0:T(8,128)S(1)} %add.210), channel_id=1, source_target_pairs={{0,2},{1,3},{2,0},{3,1},{4,6},{5,7},{6,4},{7,5},{8,10},{9,11},{10,... | collective-permute-start | bytes 12296 | tf_op jit(solution)/shard_map/ppermute | solution.py:36
  166.4 12.8 %collective-permute-start.32 = (f32[8,128]{1,0:T(8,128)S(1)}, f32[8,128]{1,0:T(8,128)S(1)}, u32[]{:S(2)}, u32[]{:S(2)}) collective-permute-start(f32[8,128]{1,0:T(8,128)S(1)} %add.210), channel_id=1, source_target_pairs={{0,3},{1,2},{2,1},{3,0},{4,7},{5,6},{6,5},{7,4},{8,11},{9,10},{10,... | collective-permute-start | bytes 12296 | tf_op jit(solution)/shard_map/ppermute | solution.py:36
  (20 other events, 97.3 us)
